TPU v7x, 32 devices: a whole 2x2x4 slice. The times are simulated.
32 devices in a mesh: walk: 16 (over z, y, x), col: 2 (over core).
Axes of the slice: x: 2, y: 2, z: 4, core: 2. Of those that a mesh axis runs over, the one named last changes fastest.
Arguments:
- jacobian: float32 [96, 32768], P('walk', 'col'), may hold values from -25 to 25
- prev_update: float32 [2, 16384], P('col', 'walk'), may hold values from -6 to 6
- base_energy: float32 [96], P('walk'), may hold values from -6 to 6
- elec_pos: float32 [96, 3, 66], P('walk'), may hold values from -8 to 8
- atom_pos: float32 [3, 21], replicated, may hold values from -6 to 6
- quad_ratio: float32 [96, 21, 66, 12], P('walk'), may hold values from -1.2 to 1.2
- rotation: int32 [96, 66], P('walk'), may hold values from 0 to 15
- channels: int32 [21], replicated, may hold values from 1 to 3
- ecp_coef: float32 [21, 3], replicated, may hold values from 0.5 to 2
- ecp_expo: float32 [21, 3], replicated, may hold values from 0.2 to 2
Outputs:
- local_energy: float32 [96], P('walk')
- update: float32 [2, 16384], P('col', 'walk')
All inputs are finite; a program needn't handle non-finite values.
Results may differ from a plain program's by a relative error of at most 0.0003.
Values sent between devices are 32-bit elements; how exact they have to be, the bound alone decides.
A program may use at most 64 MiB of HBM per device.

v0:
```python
import math

import jax
import jax.numpy as jnp
from jax import lax
from jax.sharding import PartitionSpec as P

NROT = 16


momentum = 0.9
damping = 0.1


def icosa_points():
    golden = (1.0 + math.sqrt(5.0)) / 2.0
    length = math.sqrt(1.0 + golden * golden)
    rows = []
    for first in (-1.0, 1.0):
        for second in (-golden, golden):
            rows.append((0.0, first / length, second / length))
            rows.append((first / length, second / length, 0.0))
            rows.append((second / length, 0.0, first / length))
    return jnp.asarray(rows, dtype=jnp.float32).T


def rotation_table(count):
    angle = jnp.arange(count, dtype=jnp.float32)
    turn_z = 2.0 * math.pi * angle / count
    turn_x = 0.9 * angle
    cz, sz = (jnp.cos(turn_z), jnp.sin(turn_z))
    cx, sx = (jnp.cos(turn_x), jnp.sin(turn_x))
    zeros = jnp.zeros_like(cz)
    matrix = jnp.stack(
        [
            jnp.stack([cz, -sz * cx, sz * sx], axis=-1),
            jnp.stack([sz, cz * cx, -cz * sx], axis=-1),
            jnp.stack([zeros, sx, cx], axis=-1),
        ],
        axis=1,
    )
    points = icosa_points()
    rotated = matrix[:, :, 0, None] * points[None, 0, :]
    rotated = rotated + matrix[:, :, 1, None] * points[None, 1, :]
    rotated = rotated + matrix[:, :, 2, None] * points[None, 2, :]
    return rotated.reshape(count, -1)


def nonlocal_energy(elec_pos, atom_pos, quad_ratio, rotation, channels, ecp_coef, ecp_expo):
    walkers, electrons = rotation.shape
    count = NROT
    table = rotation_table(count)
    onehot = (rotation[:, :, None] == jnp.arange(count, dtype=jnp.int32)[None, None, :]).astype(
        jnp.float32
    )
    rotated = jnp.einsum("wek,kf->wef", onehot, table, precision=lax.Precision.HIGHEST)
    rotated = rotated.reshape(walkers, electrons, 3, -1)
    diff = elec_pos[:, :, None, :] - atom_pos[None, :, :, None]
    dist2 = jnp.sum(diff * diff, axis=1)
    unit = diff / jnp.sqrt(dist2 + 0.01)[:, None, :, :]
    cosang = unit[:, 0, :, :, None] * rotated[:, None, :, 0, :]
    cosang = cosang + unit[:, 1, :, :, None] * rotated[:, None, :, 1, :]
    cosang = cosang + unit[:, 2, :, :, None] * rotated[:, None, :, 2, :]
    quad = quad_ratio.shape[-1]
    lmax = ecp_coef.shape[1]
    lower = jnp.ones_like(cosang)
    upper = cosang
    total = jnp.zeros((walkers,), jnp.float32)
    for level in range(lmax):
        if level == 0:
            poly = lower
        elif level == 1:
            poly = upper
        else:
            fresh = ((2 * level - 1) * cosang * upper - (level - 1) * lower) / level
            lower, upper = (upper, fresh)
            poly = fresh
        angular = jnp.sum(poly * quad_ratio, axis=-1) / quad
        active = (channels > level).astype(jnp.float32)
        radial = ecp_coef[None, :, level, None] * jnp.exp(-ecp_expo[None, :, level, None] * dist2)
        term = (2 * level + 1) * active[None, :, None] * radial * angular
        total = total + jnp.sum(term, axis=(1, 2))
    return total


def sum_pieces(first, second):
    first_sum, second_sum = lax.psum((first, second), ("walk", "col"))
    return (first_sum, second_sum)


def body(
    jacobian,
    prev_update,
    base_energy,
    elec_pos,
    atom_pos,
    quad_ratio,
    rotation,
    channels,
    ecp_coef,
    ecp_expo,
):
    energy_mine = base_energy + nonlocal_energy(
        elec_pos, atom_pos, quad_ratio, rotation, channels, ecp_coef, ecp_expo
    )
    columns = lax.all_to_all(jacobian, "walk", split_axis=1, concat_axis=0, tiled=True)
    walkers = columns.shape[0]
    params_total = columns.shape[1] * lax.axis_size("walk") * lax.axis_size("col")
    scale = 1.0 / params_total
    centred = columns - jnp.mean(columns, axis=0, keepdims=True)
    prev_mine = prev_update[0]
    gram_part = (
        jnp.dot(
            centred, centred.T, precision=lax.Precision.HIGHEST, preferred_element_type=jnp.float32
        )
        * scale
    )
    along_part = (
        jnp.dot(
            centred, prev_mine, precision=lax.Precision.HIGHEST, preferred_element_type=jnp.float32
        )
        * scale
    )
    extra = along_part[:, None]
    gram, extra_sum = sum_pieces(gram_part, extra)
    along = extra_sum[:, 0]
    energies = lax.all_gather(energy_mine, "walk", axis=0, tiled=True)
    eps = -(energies - jnp.mean(energies)) / math.sqrt(walkers)
    system = gram + damping * jnp.eye(walkers, dtype=jnp.float32)
    factor = jnp.linalg.cholesky(system)
    solved = jax.scipy.linalg.cho_solve((factor, True), eps - momentum * along)
    update_mine = (
        jnp.dot(
            solved, centred, precision=lax.Precision.HIGHEST, preferred_element_type=jnp.float32
        )
        + momentum * prev_mine
    )
    return (energy_mine, update_mine[None, :])


def solution(mesh):
    in_specs = (
        P("walk", "col"),
        P("col", "walk"),
        P("walk"),
        P("walk", None, None),
        P(),
        P("walk", None, None, None),
        P("walk", None),
        P(),
        P(),
        P(),
    )
    out_specs = (P("walk"), P("col", "walk"))
    return jax.shard_map(body, mesh=mesh, in_specs=in_specs, out_specs=out_specs, check_vma=False)
```

profile of v0, /device:TPU:0, one launch (start us, length us, event | category | flops | bytes accessed | tf_op | source)
XLA Modules:
  0.0 116.2 jit_solution(7199600446385334491)
XLA Ops:
  0.6 8.3 %all-to-all-start = ((f32[6,16,1024]{2,0,1:T(8,128)}), f32[6,16,1024]{2,0,1:T(8,128)S(1)}, u32[]{:S(2)}, u32[]{:S(2)}) async-start(f32[6,16,1024]{2,0,1:T(8,128)} %bitcast.95), calls=%async_computation | async-start | bytes 1048576 | tf_op jit(solution)/shard_map/all_to_all | solution.py:106
  10.2 0.3 copy-done.10
  10.8 0.1 copy.19
  10.9 0.2 fusion.12
  11.5 0.6 copy-done.11
  12.1 0.6 dynamic-slice
  13.4 0.6 multiply_reduce_fusion
  14.0 0.2 multiply_reduce_fusion.2
  14.2 0.6 copy-done.7
  14.9 0.5 fusion.33
  15.4 42.1 %all-reduce = f32[96]{0:T(128)S(1)} all-reduce(f32[96]{0:T(128)S(1)} %get-tuple-element.10), channel_id=1, replica_groups=mesh['walk'=16,'col'=2] {'walk'}, use_global_device_ids=true, to_apply=%add | all-reduce | flops 96 | bytes 768
  57.4 0.6 reduce_sum.89
  58.9 0.5 convolution_multiply_fusion
  59.4 0.2 copy-done.1
  59.6 0.4 fusion.1
  60.0 37.4 %all-reduce.1 = (f32[96,96]{1,0:T(8,128)S(1)}, f32[96,1]{0,1:T(1,128)S(1)}) all-reduce(f32[96,96]{1,0:T(8,128)S(1)} %convolution_multiply_fusion, f32[96,1]{0,1:T(1,128)S(1)} %fusion.1), channel_id=1, replica_groups=mesh['walk'=16,'col'=2] {'walk','col'}, use_global_device_ids=true, to_apply=%region_8.0 | all-reduce | flops 9312 | bytes 74496 | tf_op jit(solution)/shard_map/psum | solution.py:87
  97.5 8.8 %cholesky.16 = f32[96,96]{1,0:T(8,128)S(1)} custom-call(f32[96,96]{1,0:T(8,128)S(1)} %fusion.10), custom_call_target="Cholesky" | custom-call | tf_op jit(solution)/shard_map/jit(cholesky)/cholesky | solution.py:130
  106.3 0.6 compare_reduce_fusion
  106.9 0.7 fusion.7
  107.6 7.4 %custom-call.10 = f32[1,96,96]{1,2,0:T(8,128)S(1)} custom-call(f32[1,96,96]{2,1,0:T(8,128)S(1)} %fusion.7), custom_call_target="InvertDiagBlocksLowerTriangular" | custom-call | tf_op jit(solution)/shard_map/jit(_cho_solve)/triangular_solve | solution.py:131
  115.0 0.2 convolution_bitcast_fusion.1
  115.1 0.2 convolution_bitcast_fusion
  115.3 0.3 fusion.34
  115.6 0.6 multiply_add_fusion.1
  (68 shorter events, 2.1 us)
Async XLA Ops:
  0.6 58.1 %all-to-all-start = ((f32[6,16,1024]{2,0,1:T(8,128)}), f32[6,16,1024]{2,0,1:T(8,128)S(1)}, u32[]{:S(2)}, u32[]{:S(2)}) async-start(f32[6,16,1024]{2,0,1:T(8,128)} %bitcast.95), calls=%async_computation | async-start | bytes 1048576 | tf_op jit(solution)/shard_map/all_to_all | solution.py:106
  9.8 0.7 copy-start.10
  9.8 0.7 copy-start.9
  9.8 0.8 copy-start.8
  9.8 1.1 copy-start.4
  9.8 1.3 %copy-start.2 = (f32[6,3,66]{2,1,0:T(4,128)S(1)}, f32[6,3,66]{2,1,0:T(4,128)}, u32[]{:S(2)}) copy-start(f32[6,3,66]{2,1,0:T(4,128)} %param.14) | copy-start | bytes 14260
  9.9 1.3 %copy-start.3 = (f32[3,21]{1,0:T(4,128)S(1)}, f32[3,21]{1,0:T(4,128)}, u32[]{:S(2)}) copy-start(f32[3,21]{1,0:T(4,128)} %param.15) | copy-start | bytes 760
  9.9 3.4 %copy-start = (f32[6,21,66,12]{2,1,3,0:T(8,128)S(1)}, f32[6,21,66,12]{2,1,3,0:T(8,128)}, u32[]{:S(2)}) copy-start(f32[6,21,66,12]{2,1,3,0:T(8,128)} %param.16) | copy-start | bytes 1197508
  11.4 0.7 copy-start.11
  11.4 0.7 copy-start.12
  12.1 1.3 %copy-start.6 = (f32[21,3]{0,1:T(4,128)S(1)}, f32[21,3]{0,1:T(4,128)}, u32[]{:S(2)}) copy-start(f32[21,3]{0,1:T(4,128)} %param.19) | copy-start | bytes 760
  12.1 1.3 %copy-start.5 = (f32[21,3]{0,1:T(4,128)S(1)}, f32[21,3]{0,1:T(4,128)}, u32[]{:S(2)}) copy-start(f32[21,3]{0,1:T(4,128)} %param.20) | copy-start | bytes 760
  14.2 0.7 copy-start.7
  58.9 0.7 copy-start.1
where the time goes:
time: 117 us; the launch traced here: 116 us
  blocking collectives  79.4 us (68%)
  other arithmetic  20.7 us (18%)
  starting transfers between devices  8.32 us (7%)
  local copies, waits for them, and re-layouts  3.72 us (3%)
  between operations  2.3 us (2%)
  matrix products  1.74 us (1%)
    unnamed x1, blocking collectives  42.1 us
    psum x1, blocking collectives, sum_pieces(): first_sum, second_sum = lax.psum((first, second), ('walk', 'col'))  37.4 us
    another operation x3, other arithmetic, body(): factor = jnp.linalg.cholesky(system)  9.45 us
    all_to_all x1, starting transfers between devices, body(): lax.all_to_all(jacobian, 'walk', split_axis=1, concat_axis=0, tiled=True)  8.32 us
    another operation x2, other arithmetic, body(): solved = jax.scipy.linalg.cho_solve((factor, True), eps - momentum * along)  8.01 us
    unnamed x29, local copies, waits for them, and re-layouts  2.38 us
  transfers between devices with their start and end apart: 1, of which 0 were waited for; matrix products, arithmetic and copies ran while one was open for 4% of the time, Pallas kernels for 0%

commit v1 on v0

--- a/solution.py
+++ b/solution.py
@@ -1,8 +1,11 @@
+import functools
 import math
 
 import jax
 import jax.numpy as jnp
 from jax import lax
+from jax.experimental import pallas as pl
+from jax.experimental.pallas import tpu as pltpu
 from jax.sharding import PartitionSpec as P
 
 NROT = 16
@@ -83,12 +86,304 @@
     return total
 
 
-def sum_pieces(first, second):
-    first_sum, second_sum = lax.psum((first, second), ("walk", "col"))
-    return (first_sum, second_sum)
+MESH = pl.DeviceIdType.MESH
+PAD = 8
+
+
+def exchange_kernel(
+    n,
+    m,
+    jac_ref,
+    prev_ref,
+    energy_ref,
+    gram_ref,
+    cent_ref,
+    eall_ref,
+    cols,
+    part,
+    shares,
+    pair,
+    full,
+    ebuf,
+    jac_send,
+    jac_recv,
+    e_send,
+    e_recv,
+    rs_send,
+    rs_recv,
+    pair_send,
+    pair_recv,
+    ag_send,
+    ag_recv,
+):
+    me = lax.axis_index("walk")
+    my_col = lax.axis_index("col")
+    rows, width = cols.shape[1:]
+    walkers = rows * n
+    barrier = pltpu.get_barrier_semaphore()
+
+    def greet(s, _):
+        pl.semaphore_signal(
+            barrier, inc=1, device_id=(lax.rem(me + s, n), my_col), device_id_type=MESH
+        )
+        return 0
+
+    lax.fori_loop(1, n, greet, 0)
+    for s in range(1, m):
+        pl.semaphore_signal(
+            barrier, inc=1, device_id=(me, lax.rem(my_col + s, m)), device_id_type=MESH
+        )
+    pl.semaphore_wait(barrier, n + m - 2)
+
+    def block(index):
+        return jac_ref.at[:, pl.ds(pl.multiple_of(index * width, width), width)]
+
+    def jac_copy(s, origin):
+        other = lax.rem(me + s, n)
+        return pltpu.make_async_remote_copy(
+            src_ref=block(other),
+            dst_ref=cols.at[origin],
+            send_sem=jac_send.at[s],
+            recv_sem=jac_recv.at[origin],
+            device_id=(other, my_col),
+            device_id_type=MESH,
+        )
+
+    def tile_copy(src, dst, send, recv, s, origin):
+        other = lax.rem(me + s, n)
+        return pltpu.make_async_remote_copy(
+            src_ref=src,
+            dst_ref=dst.at[origin],
+            send_sem=send.at[s],
+            recv_sem=recv.at[origin],
+            device_id=(other, my_col),
+            device_id_type=MESH,
+        )
+
+    def start_jac(s, _):
+        jac_copy(s, me).start()
+        return 0
+
+    lax.fori_loop(1, n, start_jac, 0)
+    own = pltpu.make_async_copy(block(me), cols.at[me], jac_recv.at[me])
+    own.start()
+
+    ebuf[me] = energy_ref[...]
+
+    def start_e(s, _):
+        tile_copy(ebuf.at[me], ebuf, e_send, e_recv, s, me).start()
+        return 0
+
+    lax.fori_loop(1, n, start_e, 0)
+
+    own.wait()
+
+    def wait_jac(s, _):
+        jac_copy(s, lax.rem(me + s, n)).wait_recv()
+        return 0
+
+    lax.fori_loop(1, n, wait_jac, 0)
+
+    total = cols[0]
+    for i in range(1, n):
+        total = total + cols[i]
+    mean = jnp.sum(total, axis=0, keepdims=True) * (1.0 / walkers)
+    cent_ref[...] = jnp.zeros_like(cent_ref)
+    for i in range(n):
+        cent_ref[i, 0:rows, :] = cols[i] - mean
+    cent_ref[0, rows : rows + 1, :] = prev_ref[...]
+    cent = cent_ref[...].reshape(n * PAD, width)
+    part[...] = lax.dot_general(
+        cent,
+        cent,
+        (((1,), (1,)), ((), ())),
+        precision=lax.Precision.HIGHEST,
+        preferred_element_type=jnp.float32,
+    ).reshape(part.shape)
+
+    def start_rs(s, _):
+        tile_copy(part.at[lax.rem(me + s, n)], shares, rs_send, rs_recv, s, me).start()
+        return 0
+
+    lax.fori_loop(1, n, start_rs, 0)
+    shares[me] = part[me]
+
+    def wait_rs(s, _):
+        tile_copy(part.at[0], shares, rs_send, rs_recv, s, lax.rem(me + s, n)).wait_recv()
+        return 0
+
+    lax.fori_loop(1, n, wait_rs, 0)
+    acc = shares[0]
+    for i in range(1, n):
+        acc = acc + shares[i]
+    pair[my_col] = acc
+
+    def pair_copy(s, origin):
+        return pltpu.make_async_remote_copy(
+            src_ref=pair.at[my_col],
+            dst_ref=pair.at[origin],
+            send_sem=pair_send.at[s],
+            recv_sem=pair_recv.at[origin],
+            device_id=(me, lax.rem(my_col + s, m)),
+            device_id_type=MESH,
+        )
+
+    for s in range(1, m):
+        pair_copy(s, my_col).start()
+    for s in range(1, m):
+        pair_copy(s, lax.rem(my_col + s, m)).wait_recv()
+    acc = pair[0]
+    for c in range(1, m):
+        acc = acc + pair[c]
+    full[me] = acc
+
+    def start_ag(s, _):
+        tile_copy(full.at[me], full, ag_send, ag_recv, s, me).start()
+        return 0
+
+    lax.fori_loop(1, n, start_ag, 0)
+
+    def wait_e(s, _):
+        tile_copy(ebuf.at[me], ebuf, e_send, e_recv, s, lax.rem(me + s, n)).wait_recv()
+        return 0
+
+    lax.fori_loop(1, n, wait_e, 0)
+    eall_ref[...] = ebuf[...]
+
+    def wait_ag(s, _):
+        tile_copy(full.at[me], full, ag_send, ag_recv, s, lax.rem(me + s, n)).wait_recv()
+        return 0
+
+    lax.fori_loop(1, n, wait_ag, 0)
+    gram_ref[...] = full[...]
+
+    def wait_sends(s, _):
+        jac_copy(s, me).wait_send()
+        tile_copy(ebuf.at[me], ebuf, e_send, e_recv, s, me).wait_send()
+        tile_copy(part.at[0], shares, rs_send, rs_recv, s, me).wait_send()
+        tile_copy(full.at[me], full, ag_send, ag_recv, s, me).wait_send()
+        return 0
+
+    lax.fori_loop(1, n, wait_sends, 0)
+    for s in range(1, m):
+        pair_copy(s, my_col).wait_send()
+
+
+def exchange(n, m, jacobian, prev_update, energy_tile):
+    rows = jacobian.shape[0]
+    width = jacobian.shape[1] // n
+    wide = n * PAD
+    vmem = pl.BlockSpec(memory_space=pltpu.VMEM)
+    f32 = jnp.float32
+    dma = pltpu.SemaphoreType.DMA
+    return pl.pallas_call(
+        functools.partial(exchange_kernel, n, m),
+        out_shape=(
+            jax.ShapeDtypeStruct((n, PAD, wide), f32),
+            jax.ShapeDtypeStruct((n, PAD, width), f32),
+            jax.ShapeDtypeStruct((n, PAD, 128), f32),
+        ),
+        in_specs=[pl.BlockSpec(memory_space=pl.ANY), vmem, vmem],
+        out_specs=(vmem, vmem, vmem),
+        scratch_shapes=[
+            pltpu.VMEM((n, rows, width), f32),
+            pltpu.VMEM((n, PAD, wide), f32),
+            pltpu.VMEM((n, PAD, wide), f32),
+            pltpu.VMEM((m, PAD, wide), f32),
+            pltpu.VMEM((n, PAD, wide), f32),
+            pltpu.VMEM((n, PAD, 128), f32),
+        ]
+        + [dma((n,))] * 6
+        + [dma((m,))] * 2
+        + [dma((n,))] * 2,
+        compiler_params=pltpu.CompilerParams(
+            collective_id=0, has_side_effects=True, vmem_limit_bytes=40 * 1024 * 1024
+        ),
+    )(jacobian, prev_update, energy_tile)
+
+
+def solve_kernel(n, rows, scale, gram_ref, eall_ref, cent_ref, prev_ref, out_ref):
+    wide = n * PAD
+    walkers = n * rows
+    sub = lax.broadcasted_iota(jnp.int32, (PAD, wide), 0)
+    lane = lax.broadcasted_iota(jnp.int32, (PAD, wide), 1)
+    real_row = sub < rows
+    real = real_row & (lane % PAD < rows)
+    energies = [jnp.broadcast_to(eall_ref[i, :, 0:1], (PAD, wide)) for i in range(n)]
+    esum = energies[0]
+    for i in range(1, n):
+        esum = esum + energies[i]
+    emean = jnp.sum(jnp.where(real_row, esum, 0.0), axis=0, keepdims=True) * (1.0 / walkers)
+    panels = []
+    for i in range(n):
+        g = gram_ref[i] * scale
+        eps = -(energies[i] - emean) * (1.0 / math.sqrt(walkers))
+        along = jnp.broadcast_to(g[:, rows : rows + 1], (PAD, wide))
+        right = eps - momentum * along
+        panel = jnp.where(real, g, 0.0)
+        panel = jnp.where(real & (lane == sub + i * PAD), panel + damping, panel)
+        panels.append(jnp.where(real_row & (lane == rows), right, panel))
+
+    def spread(panel, column):
+        return jnp.broadcast_to(panel[:, column : column + 1], (PAD, wide))
+
+    for g in range(n):
+        top = panels[g]
+        marks = [spread(top, g * PAD + r) for r in range(rows)]
+        for r in range(rows):
+            inverse = 1.0 / marks[r][r : r + 1, :]
+            here = sub == r
+            factor = jnp.where(here, 0.0, marks[r])
+            line = top[r : r + 1, :] * inverse
+            top = jnp.where(here, line, top - factor * line)
+            for q in range(r + 1, rows):
+                line_q = marks[q][r : r + 1, :] * inverse
+                marks[q] = jnp.where(here, line_q, marks[q] - factor * line_q)
+        for i in range(n):
+            if i == g:
+                continue
+            panel = panels[i]
+            fresh = panel
+            for r in range(rows):
+                fresh = fresh - spread(panel, g * PAD + r) * top[r : r + 1, :]
+            panels[i] = fresh
+        panels[g] = top
+
+    width = cent_ref.shape[2]
+    acc = jnp.zeros((PAD, width), jnp.float32)
+    keep = lax.broadcasted_iota(jnp.int32, (PAD, width), 0) < rows
+    for i in range(n):
+        solved = jnp.broadcast_to(panels[i][:, rows : rows + 1], (PAD, width))
+        acc = acc + solved * cent_ref[i]
+    acc = jnp.where(keep, acc, 0.0)
+    out_ref[...] = jnp.sum(acc, axis=0, keepdims=True) + momentum * prev_ref[...]
+
+
+def solve(n, rows, scale, gram, eall, cent, prev_update):
+    if n * PAD <= 128:
+        return pl.pallas_call(
+            functools.partial(solve_kernel, n, rows, scale),
+            out_shape=jax.ShapeDtypeStruct(prev_update.shape, jnp.float32),
+            compiler_params=pltpu.CompilerParams(vmem_limit_bytes=40 * 1024 * 1024),
+        )(gram, eall, cent, prev_update)
+    walkers = n * rows
+    along = gram[:, :rows, rows].reshape(walkers) * scale
+    square = gram.reshape(n, PAD, n, PAD)[:, :rows, :, :rows].reshape(walkers, walkers) * scale
+    energies = eall[:, :rows, 0].reshape(walkers)
+    eps = -(energies - jnp.mean(energies)) / math.sqrt(walkers)
+    system = square + damping * jnp.eye(walkers, dtype=jnp.float32)
+    factor = jnp.linalg.cholesky(system)
+    solved = jax.scipy.linalg.cho_solve((factor, True), eps - momentum * along)
+    flat = cent[:, :rows, :].reshape(walkers, -1)
+    update = jnp.dot(
+        solved, flat, precision=lax.Precision.HIGHEST, preferred_element_type=jnp.float32
+    )
+    return update[None, :] + momentum * prev_update
 
 
 def body(
+    n,
+    m,
     jacobian,
     prev_update,
     base_energy,
@@ -103,39 +398,12 @@
     energy_mine = base_energy + nonlocal_energy(
         elec_pos, atom_pos, quad_ratio, rotation, channels, ecp_coef, ecp_expo
     )
-    columns = lax.all_to_all(jacobian, "walk", split_axis=1, concat_axis=0, tiled=True)
-    walkers = columns.shape[0]
-    params_total = columns.shape[1] * lax.axis_size("walk") * lax.axis_size("col")
-    scale = 1.0 / params_total
-    centred = columns - jnp.mean(columns, axis=0, keepdims=True)
-    prev_mine = prev_update[0]
-    gram_part = (
-        jnp.dot(
-            centred, centred.T, precision=lax.Precision.HIGHEST, preferred_element_type=jnp.float32
-        )
-        * scale
-    )
-    along_part = (
-        jnp.dot(
-            centred, prev_mine, precision=lax.Precision.HIGHEST, preferred_element_type=jnp.float32
-        )
-        * scale
-    )
-    extra = along_part[:, None]
-    gram, extra_sum = sum_pieces(gram_part, extra)
-    along = extra_sum[:, 0]
-    energies = lax.all_gather(energy_mine, "walk", axis=0, tiled=True)
-    eps = -(energies - jnp.mean(energies)) / math.sqrt(walkers)
-    system = gram + damping * jnp.eye(walkers, dtype=jnp.float32)
-    factor = jnp.linalg.cholesky(system)
-    solved = jax.scipy.linalg.cho_solve((factor, True), eps - momentum * along)
-    update_mine = (
-        jnp.dot(
-            solved, centred, precision=lax.Precision.HIGHEST, preferred_element_type=jnp.float32
-        )
-        + momentum * prev_mine
-    )
-    return (energy_mine, update_mine[None, :])
+    rows = jacobian.shape[0]
+    tile = jnp.zeros((PAD, 128), jnp.float32).at[:rows, :].set(energy_mine[:, None])
+    gram, cent, eall = exchange(n, m, jacobian, prev_update, tile)
+    scale = 1.0 / (jacobian.shape[1] * m)
+    update = solve(n, rows, scale, gram, eall, cent, prev_update)
+    return (energy_mine, update)
 
 
 def solution(mesh):
@@ -152,4 +420,5 @@
         P(),
     )
     out_specs = (P("walk"), P("col", "walk"))
-    return jax.shard_map(body, mesh=mesh, in_specs=in_specs, out_specs=out_specs, check_vma=False)
+    run = functools.partial(body, mesh.shape["walk"], mesh.shape["col"])
+    return jax.shard_map(run, mesh=mesh, in_specs=in_specs, out_specs=out_specs, check_vma=False)

time: 117 us -> 42.3 us (0.36)
  blocking collectives: 79.4 us -> 0 us
  Pallas kernels: 0 us -> 35.5 us
  other arithmetic: 20.7 us -> 1.42 us
  starting transfers between devices: 8.32 us -> 0 us
  matrix products: 1.74 us -> 0.21 us
  between operations: 2.3 us -> 0.84 us
    unnamed x1 -> x0, blocking collectives: 42.1 us -> none
    psum x1 -> x0, blocking collectives: 37.4 us -> none  [sum_pieces(): first_sum, second_sum = lax.psum((first, second), ('walk', 'col'))]
    pallas_call x0 -> x2, Pallas kernels: none -> 35.5 us  [the longest x1 31.8 us: exchange(): pl.pallas_call(functools.partial(exchange_kernel, n, m), out_shape=(jax.S...]
    another operation x5 -> x0, other arithmetic: 17.5 us -> none  [the longest x3 9.45 us: body(): factor = jnp.linalg.cholesky(system)]
    all_to_all x1 -> x0, starting transfers between devices: 8.32 us -> none  [body(): lax.all_to_all(jacobian, 'walk', split_axis=1, concat_axis=0, tiled=True)]
    dot_general x3 -> x0, matrix products: 1.21 us -> none  [the longest x1 0.47 us: body(): jnp.dot(centred, centred.T, precision=lax.Precision.HIGHEST, preferred_el...]
  transfers between devices with their start and end apart: 1 -> 0, of which waited for: 0 -> 0; matrix products, arithmetic and copies ran while one was open for 4% -> 0% of each run, Pallas kernels for 0% -> 0%
where the time goes in v1:
time: 42.3 us; the launch traced here: 42.1 us
  Pallas kernels  35.5 us (84%)
  local copies, waits for them, and re-layouts  4.11 us (10%)
  other arithmetic  1.42 us (3%)
  between operations  0.84 us (2%)
    pallas_call x1, Pallas kernels, exchange(): pl.pallas_call(functools.partial(exchange_kernel, n, m), out_shape=(jax.S...  31.8 us
    pallas_call x1, Pallas kernels, solve(): pl.pallas_call(functools.partial(solve_kernel, n, rows, scale), out_shape...  3.72 us
    unnamed x29, local copies, waits for them, and re-layouts  2.83 us

profile of v1, /device:TPU:0, one launch (start us, length us, event | category | flops | bytes accessed | tf_op | source)
XLA Modules:
  0.0 42.1 jit_solution(7588927886343580825)
XLA Ops:
  1.0 0.1 copy.20
  1.2 0.1 mul.343
  1.3 0.1 copy.21
  1.5 0.1 mul.351
  1.6 0.1 copy.22
  1.7 0.1 mul.359
  1.8 0.2 copy-done.11
  2.0 0.1 mul.346
  2.1 0.1 mul.354
  2.2 0.1 mul.362
  2.3 0.1 dot_general.8
  2.4 0.1 copy.18
  2.5 0.2 fusion.6
  2.8 0.1 fusion.4
  2.9 0.1 subtract_divide_fusion
  3.0 0.6 %multiply_reduce_fusion = (f32[6,21,66]{2,1,0:T(8,128)S(1)}, f32[6,21,66]{2,1,0:T(8,128)S(1)}, f32[6,21,66]{2,1,0:T(8,128)S(1)}) fusion(f32[6,21,66,12]{2,1,3,0:T(8,128)S(1)} %copy-done.2, f32[6,66,12]{1,2,0:T(8,128)S(1)} %get-tuple-element.30, f32[6,21,66]{2,1,0:T(8,128)S(1)} %get-tuple-element.27, f32[6,66,12]{1,2,0:T(8,128)S(1)} %get-tuple-element.31, ...), kind=kLoop, calls=%fused_computation.5 | loop fusion | flops 1372140 | bytes 655776 | tf_op jit(solution)/shard_map/reduce_sum | solution.py:81
  3.6 0.7 %copy-done.7 = f32[21,3]{0,1:T(4,128)S(1)} copy-done((f32[21,3]{0,1:T(4,128)S(1)}, f32[21,3]{0,1:T(4,128)}, u32[]{:S(2)}) %copy-start.7) | copy-done | bytes 276
  4.3 0.7 %copy-done.13 = s32[21]{0:T(128)S(1)} copy-done((s32[21]{0:T(128)S(1)}, s32[21]{0:T(128)}, u32[]{:S(2)}) %copy-start.13) | copy-done | bytes 108
  5.0 0.2 multiply_reduce_fusion.2
  5.2 0.6 %copy-done.8 = f32[6]{0:T(128)S(1)} copy-done((f32[6]{0:T(128)S(1)}, f32[6]{0:T(128)}, u32[]{:S(2)}) %copy-start.8) | copy-done | bytes 48
  5.9 0.5 %copy-done.12 = f32[6]{0:T(128)} copy-done((f32[6]{0:T(128)}, f32[6]{0:T(128)S(1)}, u32[]{:S(2)}) %copy-start.12) | copy-done | bytes 48
  6.5 0.1 copy-done.1
  6.6 31.8 %shard_map.122 = (f32[16,8,128]{2,1,0:T(8,128)S(1)}, f32[16,8,1024]{2,1,0:T(8,128)S(1)}, f32[16,8,128]{2,1,0:T(8,128)S(1)}) custom-call(f32[6,16384]{1,0:T(8,128)S(1)} %copy-done, f32[1,1024]{1,0:T(1,128)S(1)} %copy-done.1, f32[8,128]{1,0:T(8,128)S(1)} %scatter.8.energy_ref), custom_call_target="tpu_custom_call" | custom-call | tf_op jit(solution)/shard_map/pallas_call | solution.py:279
  38.4 3.7 %shard_map.123 = f32[1,1024]{1,0:T(1,128)} custom-call(f32[16,8,128]{2,1,0:T(8,128)S(1)} %get-tuple-element.17.gram_ref, f32[16,8,128]{2,1,0:T(8,128)S(1)} %get-tuple-element.18.eall_ref, f32[16,8,1024]{2,1,0:T(8,128)S(1)} %get-tuple-element.19.cent_ref, f32[1,1024]{1,0:T(1,128)S(1)} %copy-done.1), custom_call_target="tpu_custom_call" | custom-call | tf_op jit(solution)/shard_map/pallas_call | solution.py:364
  (49 shorter events, 0.8 us)
Async XLA Ops:
  1.4 0.7 %copy-start.11 = (f32[12]{0:T(128)S(1)}, f32[12]{0:T(128)}, u32[]{:S(2)}) copy-start(f32[12]{0:T(128)} %constant.76) | copy-start | bytes 148
  1.4 0.8 %copy-start.10 = (f32[12]{0:T(128)S(1)}, f32[12]{0:T(128)}, u32[]{:S(2)}) copy-start(f32[12]{0:T(128)} %constant.78) | copy-start | bytes 148
  1.4 0.8 %copy-start.9 = (f32[12]{0:T(128)S(1)}, f32[12]{0:T(128)}, u32[]{:S(2)}) copy-start(f32[12]{0:T(128)} %constant.80) | copy-start | bytes 148
  1.4 1.1 %copy-start.5 = (s32[6,66]{1,0:T(8,128)S(1)}, s32[6,66]{1,0:T(8,128)}, u32[]{:S(2)}) copy-start(s32[6,66]{1,0:T(8,128)} %param.19) | copy-start | bytes 4756
  1.4 1.3 %copy-start.3 = (f32[6,3,66]{2,1,0:T(4,128)S(1)}, f32[6,3,66]{2,1,0:T(4,128)}, u32[]{:S(2)}) copy-start(f32[6,3,66]{2,1,0:T(4,128)} %param.16) | copy-start | bytes 14260
  1.4 1.4 %copy-start.4 = (f32[3,21]{1,0:T(4,128)S(1)}, f32[3,21]{1,0:T(4,128)}, u32[]{:S(2)}) copy-start(f32[3,21]{1,0:T(4,128)} %param.17) | copy-start | bytes 760
  1.5 1.5 %copy-start.2 = (f32[6,21,66,12]{2,1,3,0:T(8,128)S(1)}, f32[6,21,66,12]{2,1,3,0:T(8,128)}, u32[]{:S(2)}) copy-start(f32[6,21,66,12]{2,1,3,0:T(8,128)} %param.18) | copy-start | bytes 1197508
  3.0 3.4 %copy-start = (f32[6,16384]{1,0:T(8,128)S(1)}, f32[6,16384]{1,0:T(8,128)}, u32[]{:S(2)}) copy-start(f32[6,16384]{1,0:T(8,128)} %jac_ref.1) | copy-start | bytes 1179652
  3.6 0.7 %copy-start.7 = (f32[21,3]{0,1:T(4,128)S(1)}, f32[21,3]{0,1:T(4,128)}, u32[]{:S(2)}) copy-start(f32[21,3]{0,1:T(4,128)} %param.21) | copy-start | bytes 760
  3.6 0.7 %copy-start.6 = (f32[21,3]{0,1:T(4,128)S(1)}, f32[21,3]{0,1:T(4,128)}, u32[]{:S(2)}) copy-start(f32[21,3]{0,1:T(4,128)} %param.22) | copy-start | bytes 760
  4.3 0.7 %copy-start.13 = (s32[21]{0:T(128)S(1)}, s32[21]{0:T(128)}, u32[]{:S(2)}) copy-start(s32[21]{0:T(128)} %param.20) | copy-start | bytes 256
  5.2 0.7 %copy-start.8 = (f32[6]{0:T(128)S(1)}, f32[6]{0:T(128)}, u32[]{:S(2)}) copy-start(f32[6]{0:T(128)} %param.15) | copy-start | bytes 76
  5.9 0.7 %copy-start.1 = (f32[1,1024]{1,0:T(1,128)S(1)}, f32[1,1024]{1,0:T(1,128)}, u32[]{:S(2)}) copy-start(f32[1,1024]{1,0:T(1,128)} %prev_ref.3) | copy-start | bytes 12292
  5.9 0.5 %copy-start.12 = (f32[6]{0:T(128)}, f32[6]{0:T(128)S(1)}, u32[]{:S(2)}) copy-start(f32[6]{0:T(128)S(1)} %add_add_fusion) | copy-start | bytes 76

commit v2 on v1

v2 whole, which is shorter than its diff:
```python
import functools
import math

import jax
import jax.numpy as jnp
from jax import lax
from jax.experimental import pallas as pl
from jax.experimental.pallas import tpu as pltpu
from jax.sharding import PartitionSpec as P

NROT = 16


momentum = 0.9
damping = 0.1


MESH = pl.DeviceIdType.MESH
PAD = 8


def icosa_points():
    golden = (1.0 + math.sqrt(5.0)) / 2.0
    length = math.sqrt(1.0 + golden * golden)
    rows = []
    for first in (-1.0, 1.0):
        for second in (-golden, golden):
            rows.append((0.0, first / length, second / length))
            rows.append((first / length, second / length, 0.0))
            rows.append((second / length, 0.0, first / length))
    return rows


def rotation_table(count):
    points = icosa_points()
    quad = len(points)
    angle = lax.broadcasted_iota(jnp.int32, (1, count), 1).astype(jnp.float32)
    turn_z = 2.0 * math.pi * angle / count
    turn_x = 0.9 * angle
    cz, sz = (jnp.cos(turn_z), jnp.sin(turn_z))
    cx, sx = (jnp.cos(turn_x), jnp.sin(turn_x))
    matrix = [[cz, -sz * cx, sz * sx], [sz, cz * cx, -cz * sx], [jnp.zeros_like(cz), sx, cx]]
    index = lax.broadcasted_iota(jnp.int32, (quad, count), 0)
    place = []
    for d in range(3):
        column = jnp.zeros((quad, count), jnp.float32)
        for j in range(quad):
            column = jnp.where(index == j, points[j][d], column)
        place.append(column)
    return [
        matrix[c][0] * place[0] + matrix[c][1] * place[1] + matrix[c][2] * place[2]
        for c in range(3)
    ]


def as_column(row):
    count = row.shape[1]
    index = lax.broadcasted_iota(jnp.int32, (count, count), 0)
    other = lax.broadcasted_iota(jnp.int32, (count, count), 1)
    return jnp.sum(jnp.where(index == other, row, 0.0), axis=1, keepdims=True)


def walker_energies(elec, atom, quad, rotation, channels, coef, expo, base, out):
    rows, points, atoms, electrons = quad.shape
    lmax = coef.shape[0]
    table = rotation_table(NROT)
    spot = [as_column(atom[c : c + 1, :]) for c in range(3)]
    count = as_column(channels[...].astype(jnp.float32))
    strength = [as_column(coef[level : level + 1, :]) for level in range(lmax)]
    decay = [as_column(expo[level : level + 1, :]) for level in range(lmax)]
    first = as_column(base[...])
    out[...] = jnp.zeros_like(out)
    kind = lax.broadcasted_iota(jnp.int32, (NROT, electrons), 0)

    def walker(w, _):
        onehot = (kind == rotation[pl.ds(w, 1), :]).astype(jnp.float32)
        turned = [
            jnp.dot(
                table[c], onehot, precision=lax.Precision.HIGHEST, preferred_element_type=jnp.float32
            )
            for c in range(3)
        ]
        where = elec[w]
        diff = [where[c : c + 1, :] - spot[c] for c in range(3)]
        dist2 = diff[0] * diff[0] + diff[1] * diff[1] + diff[2] * diff[2]
        root = jnp.sqrt(dist2 + 0.01)
        unit = [d / root for d in diff]
        angular = [jnp.zeros((atoms, electrons), jnp.float32) for _ in range(lmax)]
        for j in range(points):
            ratio = quad[w, j]
            cosang = unit[0] * turned[0][j : j + 1, :]
            cosang = cosang + unit[1] * turned[1][j : j + 1, :]
            cosang = cosang + unit[2] * turned[2][j : j + 1, :]
            lower, upper = None, None
            for level in range(lmax):
                if level == 0:
                    angular[0] = angular[0] + ratio
                    continue
                if level == 1:
                    lower, upper = 1.0, cosang
                else:
                    fresh = ((2 * level - 1) * cosang * upper - (level - 1) * lower) * (1.0 / level)
                    lower, upper = upper, fresh
                angular[level] = angular[level] + upper * ratio
        total = jnp.zeros((atoms, electrons), jnp.float32)
        for level in range(lmax):
            active = (count > level).astype(jnp.float32)
            radial = (strength[level] * active) * jnp.exp(-decay[level] * dist2)
            total = total + ((2 * level + 1) / points) * radial * angular[level]
        value = jnp.sum(jnp.sum(total, axis=1, keepdims=True), axis=0, keepdims=True)
        out[pl.ds(w, 1), :] = jnp.broadcast_to(value, (1, out.shape[1]))
        return 0

    lax.fori_loop(0, rows, walker, 0)
    out[0:rows, :] = out[0:rows, :] + first


def far_first(n):
    order, span = [], n
    while span > 1:
        order += [s for s in range(span // 2, n, span)]
        span //= 2
    return order + [s for s in range(1, n) if s not in order]


def step_kernel(
    n,
    m,
    finish,
    jac_ref,
    prev_ref,
    base_ref,
    elec_ref,
    atom_ref,
    quad_ref,
    rotation_ref,
    channels_ref,
    coef_ref,
    expo_ref,
    *rest,
):
    if finish:
        energy_ref, update_ref = rest[:2]
        rest = rest[2:]
        cent_ref, rest = rest[0], rest[1:]
    else:
        energy_ref, gram_ref, cent_ref = rest[:3]
        rest = rest[3:]
    (
        quad,
        cols,
        part,
        shares,
        pair,
        full,
        energies,
        quad_sem,
        jac_send,
        jac_recv,
        rs_send,
        rs_recv,
        pair_send,
        pair_recv,
        ag_send,
        ag_recv,
    ) = rest
    me = lax.axis_index("walk")
    my_col = lax.axis_index("col")
    rows, width = cols.shape[1:]
    walkers = rows * n
    scale = 1.0 / (width * n * m)
    order = far_first(n)
    fetch = pltpu.make_async_copy(quad_ref, quad, quad_sem)
    fetch.start()

    barrier = pltpu.get_barrier_semaphore()
    for s in order:
        pl.semaphore_signal(
            barrier, inc=1, device_id=(lax.rem(me + s, n), my_col), device_id_type=MESH
        )
    for s in range(1, m):
        pl.semaphore_signal(
            barrier, inc=1, device_id=(me, lax.rem(my_col + s, m)), device_id_type=MESH
        )
    pl.semaphore_wait(barrier, n + m - 2)

    def block(index):
        return jac_ref.at[:, pl.ds(pl.multiple_of(index * width, width), width)]

    def send(src, dst, send_sem, recv_sem, s):
        pltpu.make_async_remote_copy(
            src_ref=src,
            dst_ref=dst.at[me],
            send_sem=send_sem,
            recv_sem=recv_sem,
            device_id=(lax.rem(me + s, n), my_col),
            device_id_type=MESH,
        ).start()

    def wait_bytes(like, sem):
        pltpu.make_async_copy(like, like, sem).wait()

    for s in order:
        send(block(lax.rem(me + s, n)), cols, jac_send, jac_recv, s)
    pltpu.make_async_copy(block(me), cols.at[me], jac_recv).start()

    fetch.wait()
    walker_energies(
        elec_ref, atom_ref, quad, rotation_ref, channels_ref, coef_ref, expo_ref, base_ref, energies
    )
    index = lax.broadcasted_iota(jnp.int32, (rows, rows), 0)
    other = lax.broadcasted_iota(jnp.int32, (rows, rows), 1)
    energy_ref[...] = jnp.sum(
        jnp.where(index == other, energies[0:rows, 0:rows], 0.0), axis=0, keepdims=True
    )
    cent_ref[...] = jnp.zeros_like(cent_ref)
    cent_ref[0, rows : rows + 1, :] = prev_ref[...]

    wait_bytes(cols, jac_recv)
    total = cols[0]
    for i in range(1, n):
        total = total + cols[i]
    mean = jnp.sum(total, axis=0, keepdims=True) * (1.0 / walkers)
    for i in range(n):
        cent_ref[i, 0:rows, :] = cols[i] - mean
    cent = cent_ref[...].reshape(n * PAD, width)
    part[...] = lax.dot_general(
        cent,
        cent,
        (((1,), (1,)), ((), ())),
        precision=lax.Precision.HIGHEST,
        preferred_element_type=jnp.float32,
    ).reshape(part.shape)

    for s in order:
        send(part.at[lax.rem(me + s, n)], shares, rs_send, rs_recv, s)
    shares[me] = part[me]
    wait_bytes(shares.at[pl.ds(0, n - 1)], rs_recv)
    acc = shares[0]
    for i in range(1, n):
        acc = acc + shares[i]
    pair[my_col] = acc

    def pair_copy(s, origin):
        return pltpu.make_async_remote_copy(
            src_ref=pair.at[my_col],
            dst_ref=pair.at[origin],
            send_sem=pair_send.at[s],
            recv_sem=pair_recv.at[origin],
            device_id=(me, lax.rem(my_col + s, m)),
            device_id_type=MESH,
        )

    for s in range(1, m):
        pair_copy(s, my_col).start()
    for s in range(1, m):
        pair_copy(s, lax.rem(my_col + s, m)).wait_recv()
    acc = pair[0]
    for c in range(1, m):
        acc = acc + pair[c]
    lane = lax.broadcasted_iota(jnp.int32, acc.shape, 1)
    spare = jnp.broadcast_to(energies[:, 0:1], acc.shape)
    full[me] = jnp.where(lane == rows + 1, spare, acc * scale)

    for s in order:
        send(full.at[me], full, ag_send, ag_recv, s)
    wait_bytes(full.at[pl.ds(0, n - 1)], ag_recv)
    if finish:
        solve(n, rows, full, cent_ref, prev_ref, update_ref)
    else:
        gram_ref[...] = full[...]

    wait_bytes(cols.at[pl.ds(0, n - 1)], jac_send)
    wait_bytes(part.at[pl.ds(0, n - 1)], rs_send)
    wait_bytes(full.at[pl.ds(0, n - 1)], ag_send)
    for s in range(1, m):
        pair_copy(s, my_col).wait_send()


def solve(n, rows, gram_ref, cent_ref, prev_ref, out_ref):
    wide = n * PAD
    walkers = n * rows
    sub = lax.broadcasted_iota(jnp.int32, (PAD, wide), 0)
    lane = lax.broadcasted_iota(jnp.int32, (PAD, wide), 1)
    real_row = sub < rows
    real = real_row & (lane % PAD < rows)
    energies = [
        jnp.broadcast_to(gram_ref[i][:, rows + 1 : rows + 2], (PAD, wide)) for i in range(n)
    ]
    esum = energies[0]
    for i in range(1, n):
        esum = esum + energies[i]
    emean = jnp.sum(jnp.where(real_row, esum, 0.0), axis=0, keepdims=True) * (1.0 / walkers)
    panels = []
    for i in range(n):
        g = gram_ref[i]
        eps = -(energies[i] - emean) * (1.0 / math.sqrt(walkers))
        along = jnp.broadcast_to(g[:, rows : rows + 1], (PAD, wide))
        right = eps - momentum * along
        panel = jnp.where(real, g, 0.0)
        panel = jnp.where(real & (lane == sub + i * PAD), panel + damping, panel)
        panels.append(jnp.where(real_row & (lane == rows), right, panel))

    def spread(panel, column):
        return jnp.broadcast_to(panel[:, column : column + 1], (PAD, wide))

    for g in range(n):
        top = panels[g]
        marks = [spread(top, g * PAD + r) for r in range(rows)]
        for r in range(rows):
            inverse = 1.0 / marks[r][r : r + 1, :]
            here = sub == r
            factor = jnp.where(here, 0.0, marks[r])
            line = top[r : r + 1, :] * inverse
            top = jnp.where(here, line, top - factor * line)
            for q in range(r + 1, rows):
                line_q = marks[q][r : r + 1, :] * inverse
                marks[q] = jnp.where(here, line_q, marks[q] - factor * line_q)
        for i in range(n):
            if i == g:
                continue
            panel = panels[i]
            fresh = panel
            for r in range(rows):
                fresh = fresh - spread(panel, g * PAD + r) * top[r : r + 1, :]
            panels[i] = fresh
        panels[g] = top

    width = cent_ref.shape[2]
    acc = jnp.zeros((PAD, width), jnp.float32)
    keep = lax.broadcasted_iota(jnp.int32, (PAD, width), 0) < rows
    for i in range(n):
        solved = jnp.broadcast_to(panels[i][:, rows : rows + 1], (PAD, width))
        acc = acc + solved * cent_ref[i]
    acc = jnp.where(keep, acc, 0.0)
    out_ref[...] = jnp.sum(acc, axis=0, keepdims=True) + momentum * prev_ref[...]


def step(n, m, prev_update, jacobian, base, elec_pos, atom_pos, quad, rotation, channels, coef, expo):
    rows = jacobian.shape[0]
    width = jacobian.shape[1] // n
    wide = n * PAD
    finish = wide <= 128
    vmem = pl.BlockSpec(memory_space=pltpu.VMEM)
    anywhere = pl.BlockSpec(memory_space=pl.ANY)
    f32 = jnp.float32
    dma = pltpu.SemaphoreType.DMA
    gram = jax.ShapeDtypeStruct((n, PAD, wide), f32)
    cent = jax.ShapeDtypeStruct((n, PAD, width), f32)
    out_shape = [jax.ShapeDtypeStruct((1, rows), f32)]
    scratch = []
    if finish:
        out_shape += [jax.ShapeDtypeStruct(prev_update.shape, f32)]
        scratch += [pltpu.VMEM(cent.shape, f32)]
    else:
        out_shape += [gram, cent]
    return pl.pallas_call(
        functools.partial(step_kernel, n, m, finish),
        out_shape=out_shape,
        in_specs=[anywhere] + [vmem] * 4 + [anywhere] + [vmem] * 4,
        out_specs=[vmem] * len(out_shape),
        scratch_shapes=scratch
        + [
            pltpu.VMEM(quad.shape, f32),
            pltpu.VMEM((n, rows, width), f32),
            pltpu.VMEM(gram.shape, f32),
            pltpu.VMEM(gram.shape, f32),
            pltpu.VMEM((m, PAD, wide), f32),
            pltpu.VMEM(gram.shape, f32),
            pltpu.VMEM((PAD, 128), f32),
        ]
        + [dma] * 5
        + [dma((m,))] * 2
        + [dma] * 2,
        compiler_params=pltpu.CompilerParams(
            collective_id=0, has_side_effects=True, vmem_limit_bytes=40 * 1024 * 1024
        ),
    )(jacobian, prev_update, base, elec_pos, atom_pos, quad, rotation, channels, coef, expo)


def finish_outside(n, rows, gram, cent, prev_update):
    walkers = n * rows
    along = gram[:, :rows, rows].reshape(walkers)
    energies = gram[:, :rows, rows + 1].reshape(walkers)
    square = gram.reshape(n, PAD, n, PAD)[:, :rows, :, :rows].reshape(walkers, walkers)
    eps = -(energies - jnp.mean(energies)) / math.sqrt(walkers)
    system = square + damping * jnp.eye(walkers, dtype=jnp.float32)
    factor = jnp.linalg.cholesky(system)
    solved = jax.scipy.linalg.cho_solve((factor, True), eps - momentum * along)
    flat = cent[:, :rows, :].reshape(walkers, -1)
    update = jnp.dot(
        solved, flat, precision=lax.Precision.HIGHEST, preferred_element_type=jnp.float32
    )
    return update[None, :] + momentum * prev_update


def body(
    n,
    m,
    jacobian,
    prev_update,
    base_energy,
    elec_pos,
    atom_pos,
    quad_ratio,
    rotation,
    channels,
    ecp_coef,
    ecp_expo,
):
    rows = jacobian.shape[0]
    energy, *rest = step(
        n,
        m,
        prev_update,
        jacobian,
        base_energy.reshape(1, -1),
        elec_pos,
        atom_pos,
        jnp.transpose(quad_ratio, (0, 3, 1, 2)),
        rotation,
        channels.reshape(1, -1),
        ecp_coef.T,
        ecp_expo.T,
    )
    if len(rest) == 1:
        update = rest[0]
    else:
        update = finish_outside(n, rows, *rest, prev_update)
    return (energy.reshape(rows), update)


def solution(mesh):
    in_specs = (
        P("walk", "col"),
        P("col", "walk"),
        P("walk"),
        P("walk", None, None),
        P(),
        P("walk", None, None, None),
        P("walk", None),
        P(),
        P(),
        P(),
    )
    out_specs = (P("walk"), P("col", "walk"))
    run = functools.partial(body, mesh.shape["walk"], mesh.shape["col"])
    return jax.shard_map(run, mesh=mesh, in_specs=in_specs, out_specs=out_specs, check_vma=False)
```

time: 42.3 us -> 39.9 us (0.943)
  Pallas kernels: 35.5 us -> 32.1 us
  local copies, waits for them, and re-layouts: 4.11 us -> 6.74 us
  other arithmetic: 1.42 us -> 0 us
    unnamed x29 -> x22, local copies, waits for them, and re-layouts: 2.83 us -> 6.74 us
    pallas_call x2 -> x1, Pallas kernels: 35.5 us -> 32.1 us  [step(): pl.pallas_call(functools.partial(step_kernel, n, m, finish), out_shape=ou...]
    mul x17 -> x0, local copies, waits for them, and re-layouts: 1.02 us -> none  [the longest x5 0.33 us: rotation_table(): rotated = rotated + matrix[:, :, 2, None] * points[None, 2, :]]
    reduce_sum x3 -> x0, other arithmetic: 0.9 us -> none  [the longest x1 0.56 us: nonlocal_energy(): angular = jnp.sum(poly * quad_ratio, axis=-1) / quad]
where the time goes in v2:
time: 39.9 us; the launch traced here: 39.5 us
  Pallas kernels  32.1 us (80%)
  local copies, waits for them, and re-layouts  6.74 us (17%)
  between operations  0.68 us (2%)
    pallas_call x1, Pallas kernels, step(): pl.pallas_call(functools.partial(step_kernel, n, m, finish), out_shape=ou...  32.1 us
    unnamed x22, local copies, waits for them, and re-layouts  6.74 us

profile of v2, /device:TPU:0, one launch (start us, length us, event | category | flops | bytes accessed | tf_op | source)
XLA Modules:
  0.0 39.5 jit_solution(8058372575761923987)
XLA Ops:
  0.6 0.0 copy-start.4
  0.6 0.0 copy-start.3
  0.7 0.0 copy-start.8
  0.7 0.0 copy-start.9
  0.7 0.6 %copy-done.4 = s32[6,66]{1,0:T(8,128)S(1)} copy-done((s32[6,66]{1,0:T(8,128)S(1)}, s32[6,66]{1,0:T(8,128)}, u32[]{:S(2)}) %copy-start.4) | copy-done | bytes 1608
  1.3 0.0 copy-done.3
  1.3 0.0 copy-done.8
  1.3 0.0 copy-done.9
  1.3 0.0 copy-start
  1.3 1.2 %copy-done = f32[6,21,66,12]{2,1,3,0:T(8,128)S(1)} copy-done((f32[6,21,66,12]{2,1,3,0:T(8,128)S(1)}, f32[6,21,66,12]{2,1,3,0:T(8,128)}, u32[]{:S(2)}) %copy-start) | copy-done | bytes 399192
  2.5 0.0 copy-start.1
  2.5 1.0 %copy-done.1 = f32[6,16384]{1,0:T(8,128)S(1)} copy-done((f32[6,16384]{1,0:T(8,128)S(1)}, f32[6,16384]{1,0:T(8,128)}, u32[]{:S(2)}) %copy-start.1) | copy-done | bytes 393240
  3.6 0.0 copy-start.2
  3.6 0.7 %copy-done.2 = f32[6,3,66]{2,1,0:T(4,128)S(1)} copy-done((f32[6,3,66]{2,1,0:T(4,128)S(1)}, f32[6,3,66]{2,1,0:T(4,128)}, u32[]{:S(2)}) %copy-start.2) | copy-done | bytes 4776
  4.3 0.0 copy-start.5
  4.3 0.7 %copy-done.5 = f32[3,21]{1,0:T(4,128)S(1)} copy-done((f32[3,21]{1,0:T(4,128)S(1)}, f32[3,21]{1,0:T(4,128)}, u32[]{:S(2)}) %copy-start.5) | copy-done | bytes 276
  4.9 0.0 copy-start.6
  4.9 0.7 %copy-done.6 = f32[21,3]{0,1:T(4,128)S(1)} copy-done((f32[21,3]{0,1:T(4,128)S(1)}, f32[21,3]{0,1:T(4,128)}, u32[]{:S(2)}) %copy-start.6) | copy-done | bytes 276
  5.6 0.0 copy-start.7
  5.6 0.7 %copy-done.7 = f32[21,3]{0,1:T(4,128)S(1)} copy-done((f32[21,3]{0,1:T(4,128)S(1)}, f32[21,3]{0,1:T(4,128)}, u32[]{:S(2)}) %copy-start.7) | copy-done | bytes 276
  6.3 32.1 %shard_map.113 = (f32[1,6]{1,0:T(1,128)S(1)}, f32[1,1024]{1,0:T(1,128)S(1)}) custom-call(f32[6,16384]{1,0:T(8,128)S(1)} %copy-done.1, f32[1,1024]{1,0:T(1,128)S(1)} %copy-done.3, f32[1,6]{1,0:T(1,128)S(1)} %bitcast.9, f32[6,3,66]{2,1,0:T(4,128)S(1)} %copy-done.2, f32[3,21]{1,0:T(4,128)S(1)} %copy-done.5, f32[6,12,21,66]{3,2,1,0:T(8,128)S(1)} %bitcast.6, ...), custom_call_target="tpu_custom_call" | custom-call | tf_op jit(solution)/shard_map/pallas_call | solution.py:357
  38.4 0.5 %copy.14 = f32[6]{0:T(128)} copy(f32[6]{0:T(128)S(1)} %bitcast.11) | data formatting | bytes 48
  38.9 0.6 %copy.15 = f32[1,1024]{1,0:T(1,128)} copy(f32[1,1024]{1,0:T(1,128)S(1)} %get-tuple-element.9) | data formatting | bytes 8192
Async XLA Ops:
  0.6 0.7 %copy-start.4 = (s32[6,66]{1,0:T(8,128)S(1)}, s32[6,66]{1,0:T(8,128)}, u32[]{:S(2)}) copy-start(s32[6,66]{1,0:T(8,128)} %rotation_ref.1) | copy-start | bytes 4756
  0.6 0.7 %copy-start.3 = (f32[1,1024]{1,0:T(1,128)S(1)}, f32[1,1024]{1,0:T(1,128)}, u32[]{:S(2)}) copy-start(f32[1,1024]{1,0:T(1,128)} %prev_ref.1) | copy-start | bytes 12292
  0.7 0.7 %copy-start.8 = (f32[6]{0:T(128)S(1)}, f32[6]{0:T(128)}, u32[]{:S(2)}) copy-start(f32[6]{0:T(128)} %param.12) | copy-start | bytes 76
  0.7 0.7 %copy-start.9 = (s32[21]{0:T(128)S(1)}, s32[21]{0:T(128)}, u32[]{:S(2)}) copy-start(s32[21]{0:T(128)} %param.17) | copy-start | bytes 256
  1.3 1.2 %copy-start = (f32[6,21,66,12]{2,1,3,0:T(8,128)S(1)}, f32[6,21,66,12]{2,1,3,0:T(8,128)}, u32[]{:S(2)}) copy-start(f32[6,21,66,12]{2,1,3,0:T(8,128)} %param.15) | copy-start | bytes 1197508
  2.5 1.0 %copy-start.1 = (f32[6,16384]{1,0:T(8,128)S(1)}, f32[6,16384]{1,0:T(8,128)}, u32[]{:S(2)}) copy-start(f32[6,16384]{1,0:T(8,128)} %jac_ref.1) | copy-start | bytes 1179652
  3.6 0.7 %copy-start.2 = (f32[6,3,66]{2,1,0:T(4,128)S(1)}, f32[6,3,66]{2,1,0:T(4,128)}, u32[]{:S(2)}) copy-start(f32[6,3,66]{2,1,0:T(4,128)} %elec_ref.1) | copy-start | bytes 14260
  4.3 0.7 %copy-start.5 = (f32[3,21]{1,0:T(4,128)S(1)}, f32[3,21]{1,0:T(4,128)}, u32[]{:S(2)}) copy-start(f32[3,21]{1,0:T(4,128)} %atom_ref.1) | copy-start | bytes 760
  4.9 0.7 %copy-start.6 = (f32[21,3]{0,1:T(4,128)S(1)}, f32[21,3]{0,1:T(4,128)}, u32[]{:S(2)}) copy-start(f32[21,3]{0,1:T(4,128)} %param.18) | copy-start | bytes 760
  5.6 0.7 %copy-start.7 = (f32[21,3]{0,1:T(4,128)S(1)}, f32[21,3]{0,1:T(4,128)}, u32[]{:S(2)}) copy-start(f32[21,3]{0,1:T(4,128)} %param.19) | copy-start | bytes 760

commit v3 on v2

--- a/solution.py
+++ b/solution.py
@@ -17,6 +17,7 @@
 
 MESH = pl.DeviceIdType.MESH
 PAD = 8
+CHUNKS = 2
 
 
 def icosa_points():
@@ -137,42 +138,41 @@
     channels_ref,
     coef_ref,
     expo_ref,
-    *rest,
+    energy_ref,
+    result_ref,
+    cent_ref,
+    prev,
+    base,
+    elec,
+    atom,
+    quad,
+    rotation,
+    channels,
+    coef,
+    expo,
+    cols,
+    part,
+    shares,
+    pair,
+    full,
+    energies,
+    fetch_sem,
+    jac_send,
+    jac_recv,
+    rs_send,
+    rs_recv,
+    pair_send,
+    pair_recv,
+    ag_send,
+    ag_recv,
 ):
-    if finish:
-        energy_ref, update_ref = rest[:2]
-        rest = rest[2:]
-        cent_ref, rest = rest[0], rest[1:]
-    else:
-        energy_ref, gram_ref, cent_ref = rest[:3]
-        rest = rest[3:]
-    (
-        quad,
-        cols,
-        part,
-        shares,
-        pair,
-        full,
-        energies,
-        quad_sem,
-        jac_send,
-        jac_recv,
-        rs_send,
-        rs_recv,
-        pair_send,
-        pair_recv,
-        ag_send,
-        ag_recv,
-    ) = rest
     me = lax.axis_index("walk")
     my_col = lax.axis_index("col")
-    rows, width = cols.shape[1:]
+    chunks, _, rows, span = cols.shape
+    width = chunks * span
     walkers = rows * n
     scale = 1.0 / (width * n * m)
     order = far_first(n)
-    fetch = pltpu.make_async_copy(quad_ref, quad, quad_sem)
-    fetch.start()
-
     barrier = pltpu.get_barrier_semaphore()
     for s in order:
         pl.semaphore_signal(
@@ -182,10 +182,28 @@
         pl.semaphore_signal(
             barrier, inc=1, device_id=(me, lax.rem(my_col + s, m)), device_id_type=MESH
         )
+    sources = (
+        quad_ref,
+        prev_ref,
+        base_ref,
+        elec_ref,
+        atom_ref,
+        rotation_ref,
+        channels_ref,
+        coef_ref,
+        expo_ref,
+    )
+    targets = (quad, prev, base, elec, atom, rotation, channels, coef, expo)
+    fetches = [
+        pltpu.make_async_copy(source, target, fetch_sem.at[k])
+        for k, (source, target) in enumerate(zip(sources, targets))
+    ]
+    for fetch in fetches:
+        fetch.start()
     pl.semaphore_wait(barrier, n + m - 2)
 
-    def block(index):
-        return jac_ref.at[:, pl.ds(pl.multiple_of(index * width, width), width)]
+    def block(index, k):
+        return jac_ref.at[:, pl.ds(pl.multiple_of(index * width + k * span, span), span)]
 
     def send(src, dst, send_sem, recv_sem, s):
         pltpu.make_async_remote_copy(
@@ -200,37 +218,36 @@
     def wait_bytes(like, sem):
         pltpu.make_async_copy(like, like, sem).wait()
 
-    for s in order:
-        send(block(lax.rem(me + s, n)), cols, jac_send, jac_recv, s)
-    pltpu.make_async_copy(block(me), cols.at[me], jac_recv).start()
-
-    fetch.wait()
-    walker_energies(
-        elec_ref, atom_ref, quad, rotation_ref, channels_ref, coef_ref, expo_ref, base_ref, energies
-    )
-    index = lax.broadcasted_iota(jnp.int32, (rows, rows), 0)
-    other = lax.broadcasted_iota(jnp.int32, (rows, rows), 1)
-    energy_ref[...] = jnp.sum(
-        jnp.where(index == other, energies[0:rows, 0:rows], 0.0), axis=0, keepdims=True
-    )
+    for k in range(chunks):
+        for s in order:
+            send(block(lax.rem(me + s, n), k), cols.at[k], jac_send.at[k], jac_recv.at[k], s)
+        pltpu.make_async_copy(block(me, k), cols.at[k, me], jac_recv.at[k]).start()
+
+    for fetch in fetches:
+        fetch.wait()
+    walker_energies(elec, atom, quad, rotation, channels, coef, expo, base, energies)
     cent_ref[...] = jnp.zeros_like(cent_ref)
-    cent_ref[0, rows : rows + 1, :] = prev_ref[...]
-
-    wait_bytes(cols, jac_recv)
-    total = cols[0]
-    for i in range(1, n):
-        total = total + cols[i]
-    mean = jnp.sum(total, axis=0, keepdims=True) * (1.0 / walkers)
-    for i in range(n):
-        cent_ref[i, 0:rows, :] = cols[i] - mean
-    cent = cent_ref[...].reshape(n * PAD, width)
-    part[...] = lax.dot_general(
-        cent,
-        cent,
-        (((1,), (1,)), ((), ())),
-        precision=lax.Precision.HIGHEST,
-        preferred_element_type=jnp.float32,
-    ).reshape(part.shape)
+    cent_ref[0, rows : rows + 1, :] = prev[...]
+
+    gram = None
+    for k in range(chunks):
+        wait_bytes(cols.at[k], jac_recv.at[k])
+        total = cols[k, 0]
+        for i in range(1, n):
+            total = total + cols[k, i]
+        mean = jnp.sum(total, axis=0, keepdims=True) * (1.0 / walkers)
+        for i in range(n):
+            cent_ref[i, 0:rows, k * span : (k + 1) * span] = cols[k, i] - mean
+        cent = cent_ref[:, :, k * span : (k + 1) * span].reshape(n * PAD, span)
+        piece = lax.dot_general(
+            cent,
+            cent,
+            (((1,), (1,)), ((), ())),
+            precision=lax.Precision.HIGHEST,
+            preferred_element_type=jnp.float32,
+        )
+        gram = piece if gram is None else gram + piece
+    part[...] = gram.reshape(part.shape)
 
     for s in order:
         send(part.at[lax.rem(me + s, n)], shares, rs_send, rs_recv, s)
@@ -266,18 +283,25 @@
         send(full.at[me], full, ag_send, ag_recv, s)
     wait_bytes(full.at[pl.ds(0, n - 1)], ag_recv)
     if finish:
-        solve(n, rows, full, cent_ref, prev_ref, update_ref)
+        solve(n, rows, full, cent_ref, prev, energies, result_ref, energy_ref)
     else:
-        gram_ref[...] = full[...]
-
-    wait_bytes(cols.at[pl.ds(0, n - 1)], jac_send)
+        result_ref[...] = full[...]
+        energy_ref[...] = jnp.broadcast_to(energies[0:rows, 0:1], (rows, 128))
+
+    for k in range(chunks):
+        wait_bytes(cols.at[k, pl.ds(0, n - 1)], jac_send.at[k])
     wait_bytes(part.at[pl.ds(0, n - 1)], rs_send)
     wait_bytes(full.at[pl.ds(0, n - 1)], ag_send)
     for s in range(1, m):
         pair_copy(s, my_col).wait_send()
 
 
-def solve(n, rows, gram_ref, cent_ref, prev_ref, out_ref):
+def solve(n, rows, gram_ref, cent_ref, prev_ref, energy_ref, out_ref, mine_ref):
+    index = lax.broadcasted_iota(jnp.int32, (rows, rows), 0)
+    other = lax.broadcasted_iota(jnp.int32, (rows, rows), 1)
+    mine_ref[...] = jnp.sum(
+        jnp.where(index == other, energy_ref[0:rows, 0:rows], 0.0), axis=0, keepdims=True
+    )
     wide = n * PAD
     walkers = n * rows
     sub = lax.broadcasted_iota(jnp.int32, (PAD, wide), 0)
@@ -336,46 +360,43 @@
     out_ref[...] = jnp.sum(acc, axis=0, keepdims=True) + momentum * prev_ref[...]
 
 
-def step(n, m, prev_update, jacobian, base, elec_pos, atom_pos, quad, rotation, channels, coef, expo):
+def step(n, m, jacobian, prev_update, base, elec_pos, atom_pos, quad, rotation, channels, coef, expo):
     rows = jacobian.shape[0]
     width = jacobian.shape[1] // n
     wide = n * PAD
-    finish = wide <= 128
     vmem = pl.BlockSpec(memory_space=pltpu.VMEM)
-    anywhere = pl.BlockSpec(memory_space=pl.ANY)
+    hbm = pl.BlockSpec(memory_space=pltpu.HBM)
     f32 = jnp.float32
     dma = pltpu.SemaphoreType.DMA
-    gram = jax.ShapeDtypeStruct((n, PAD, wide), f32)
-    cent = jax.ShapeDtypeStruct((n, PAD, width), f32)
-    out_shape = [jax.ShapeDtypeStruct((1, rows), f32)]
-    scratch = []
+    small = (prev_update, base, elec_pos, atom_pos, quad, rotation, channels, coef, expo)
+    finish = wide <= 128
+    gram = (n, PAD, wide)
+    cent = (n, PAD, width)
+    scratch = [pltpu.VMEM(x.shape, x.dtype) for x in small]
     if finish:
-        out_shape += [jax.ShapeDtypeStruct(prev_update.shape, f32)]
-        scratch += [pltpu.VMEM(cent.shape, f32)]
+        shapes = [(1, rows), prev_update.shape]
+        scratch = [pltpu.VMEM(cent, f32)] + scratch
     else:
-        out_shape += [gram, cent]
+        shapes = [(rows, 128), gram, cent]
     return pl.pallas_call(
         functools.partial(step_kernel, n, m, finish),
-        out_shape=out_shape,
-        in_specs=[anywhere] + [vmem] * 4 + [anywhere] + [vmem] * 4,
-        out_specs=[vmem] * len(out_shape),
+        out_shape=[jax.ShapeDtypeStruct(shape, f32) for shape in shapes],
+        in_specs=[hbm] * 10,
+        out_specs=[vmem] * len(shapes),
         scratch_shapes=scratch
         + [
-            pltpu.VMEM(quad.shape, f32),
-            pltpu.VMEM((n, rows, width), f32),
-            pltpu.VMEM(gram.shape, f32),
-            pltpu.VMEM(gram.shape, f32),
+            pltpu.VMEM((CHUNKS, n, rows, width // CHUNKS), f32),
+            pltpu.VMEM(gram, f32),
+            pltpu.VMEM(gram, f32),
             pltpu.VMEM((m, PAD, wide), f32),
-            pltpu.VMEM(gram.shape, f32),
+            pltpu.VMEM(gram, f32),
             pltpu.VMEM((PAD, 128), f32),
         ]
-        + [dma] * 5
+        + [dma((len(small),)), dma((CHUNKS,)), dma((CHUNKS,)), dma, dma]
         + [dma((m,))] * 2
         + [dma] * 2,
-        compiler_params=pltpu.CompilerParams(
-            collective_id=0, has_side_effects=True, vmem_limit_bytes=40 * 1024 * 1024
-        ),
-    )(jacobian, prev_update, base, elec_pos, atom_pos, quad, rotation, channels, coef, expo)
+        compiler_params=pltpu.CompilerParams(collective_id=0, has_side_effects=True, vmem_limit_bytes=60 * 1024 * 1024),
+    )(jacobian, *small)
 
 
 def finish_outside(n, rows, gram, cent, prev_update):
@@ -409,11 +430,11 @@
     ecp_expo,
 ):
     rows = jacobian.shape[0]
-    energy, *rest = step(
+    energy, result, *cent = step(
         n,
         m,
+        jacobian,
         prev_update,
-        jacobian,
         base_energy.reshape(1, -1),
         elec_pos,
         atom_pos,
@@ -423,11 +444,9 @@
         ecp_coef.T,
         ecp_expo.T,
     )
-    if len(rest) == 1:
-        update = rest[0]
-    else:
-        update = finish_outside(n, rows, *rest, prev_update)
-    return (energy.reshape(rows), update)
+    if cent:
+        return (energy[:, 0], finish_outside(n, rows, result, cent[0], prev_update))
+    return (energy.reshape(rows), result)
 
 
 def solution(mesh):

time: 39.9 us -> 35.8 us (0.90)
  local copies, waits for them, and re-layouts: 6.74 us -> 1.74 us
  Pallas kernels: 32.1 us -> 33.2 us
    unnamed x22 -> x6, local copies, waits for them, and re-layouts: 6.74 us -> 1.74 us
    pallas_call x1, Pallas kernels: 32.1 us -> 33.2 us  [step(): pl.pallas_call(functools.partial(step_kernel, n, m, finish), out_shape=[j...]
where the time goes in v3:
time: 35.8 us; the launch traced here: 35.6 us
  Pallas kernels  33.2 us (93%)
  local copies, waits for them, and re-layouts  1.74 us (5%)
  between operations  0.66 us (2%)
    pallas_call x1, Pallas kernels, step(): pl.pallas_call(functools.partial(step_kernel, n, m, finish), out_shape=[j...  33.2 us
    unnamed x6, local copies, waits for them, and re-layouts  1.74 us

profile of v3, /device:TPU:0, one launch (start us, length us, event | category | flops | bytes accessed | tf_op | source)
XLA Modules:
  0.0 35.6 jit_solution(7570710980726363682)
XLA Ops:
  0.6 33.2 %shard_map.113 = (f32[1,6]{1,0:T(1,128)}, f32[1,1024]{1,0:T(1,128)}) custom-call(f32[6,16384]{1,0:T(8,128)} %jac_ref.1, f32[1,1024]{1,0:T(1,128)} %prev_ref.1, f32[1,6]{1,0:T(1,128)} %bitcast.9, f32[6,3,66]{2,1,0:T(4,128)} %elec_ref.1, f32[3,21]{1,0:T(4,128)} %atom_ref.1, f32[6,12,21,66]{3,2,1,0:T(8,128)} %bitcast.6, s32[6,66]{1,0:T(8,128)} %rotation_ref.1, ...), custom_call_target="tpu_custom_call" | custom-call | tf_op jit(solution)/shard_map/pallas_call | solution.py:381
  33.9 0.0 copy-start
  33.9 0.0 copy-start.1
  33.9 0.6 %copy-done.1 = f32[1,6]{1,0:T(1,128)S(1)} copy-done((f32[1,6]{1,0:T(1,128)S(1)}, f32[1,6]{1,0:T(1,128)}, u32[]{:S(2)}) %copy-start.1) | copy-done | bytes 48
  34.5 0.5 %copy.14 = f32[6]{0:T(128)} copy(f32[6]{0:T(128)S(1)} %bitcast.11) | data formatting | bytes 48
  35.0 0.0 copy-done
  35.0 0.6 %copy.15 = f32[1,1024]{1,0:T(1,128)} copy(f32[1,1024]{1,0:T(1,128)S(1)} %copy-done) | data formatting | bytes 8192
Async XLA Ops:
  33.9 1.2 %copy-start = (f32[1,1024]{1,0:T(1,128)S(1)}, f32[1,1024]{1,0:T(1,128)}, u32[]{:S(2)}) copy-start(f32[1,1024]{1,0:T(1,128)} %get-tuple-element.9) | copy-start | bytes 12292
  33.9 0.6 %copy-start.1 = (f32[1,6]{1,0:T(1,128)S(1)}, f32[1,6]{1,0:T(1,128)}, u32[]{:S(2)}) copy-start(f32[1,6]{1,0:T(1,128)} %get-tuple-element.4) | copy-start | bytes 76

commit v4 on v3

--- a/solution.py
+++ b/solution.py
@@ -61,7 +61,7 @@
     return jnp.sum(jnp.where(index == other, row, 0.0), axis=1, keepdims=True)
 
 
-def walker_energies(elec, atom, quad, rotation, channels, coef, expo, base, out):
+def walker_energies(share, begin, elec, atom, quad, rotation, channels, coef, expo, base, out):
     rows, points, atoms, electrons = quad.shape
     lmax = coef.shape[0]
     table = rotation_table(NROT)
@@ -73,7 +73,8 @@
     out[...] = jnp.zeros_like(out)
     kind = lax.broadcasted_iota(jnp.int32, (NROT, electrons), 0)
 
-    def walker(w, _):
+    def walker(k, _):
+        w = lax.rem(begin + k, rows)
         onehot = (kind == rotation[pl.ds(w, 1), :]).astype(jnp.float32)
         turned = [
             jnp.dot(
@@ -112,8 +113,10 @@
         out[pl.ds(w, 1), :] = jnp.broadcast_to(value, (1, out.shape[1]))
         return 0
 
-    lax.fori_loop(0, rows, walker, 0)
-    out[0:rows, :] = out[0:rows, :] + first
+    lax.fori_loop(0, share, walker, 0)
+    place = lax.broadcasted_iota(jnp.int32, (rows, out.shape[1]), 0)
+    mine = (place >= begin) & (place < begin + share)
+    out[0:rows, :] = jnp.where(mine, out[0:rows, :] + first, 0.0)
 
 
 def far_first(n):
@@ -122,6 +125,17 @@
         order += [s for s in range(span // 2, n, span)]
         span //= 2
     return order + [s for s in range(1, n) if s not in order]
+
+
+def plane_of(n, m):
+    flat = 4 if n % 4 == 0 else 1
+    while n % (flat * m) != 0:
+        flat -= 1
+    return flat
+
+
+def spread_energy(full, me, rows):
+    return jnp.broadcast_to(full[me][0:rows, rows + 1 : rows + 2], (rows, 128))
 
 
 def step_kernel(
@@ -153,7 +167,7 @@
     cols,
     part,
     shares,
-    pair,
+    lines,
     full,
     energies,
     fetch_sem,
@@ -161,8 +175,8 @@
     jac_recv,
     rs_send,
     rs_recv,
-    pair_send,
-    pair_recv,
+    line_send,
+    line_recv,
     ag_send,
     ag_recv,
 ):
@@ -173,15 +187,27 @@
     walkers = rows * n
     scale = 1.0 / (width * n * m)
     order = far_first(n)
+    flat = plane_of(n, m)
+    plane = flat * m
+    groups = n // plane
+    layer = me // flat
+    inner = lax.rem(me, flat)
+    rank = inner * m + my_col
+    own = pl.ds(rank * groups, groups)
+
     barrier = pltpu.get_barrier_semaphore()
     for s in order:
         pl.semaphore_signal(
             barrier, inc=1, device_id=(lax.rem(me + s, n), my_col), device_id_type=MESH
         )
-    for s in range(1, m):
-        pl.semaphore_signal(
-            barrier, inc=1, device_id=(me, lax.rem(my_col + s, m)), device_id_type=MESH
-        )
+    for s in range(flat):
+        for t in range(1, m):
+            pl.semaphore_signal(
+                barrier,
+                inc=1,
+                device_id=(layer * flat + lax.rem(inner + s, flat), lax.rem(my_col + t, m)),
+                device_id_type=MESH,
+            )
     sources = (
         quad_ref,
         prev_ref,
@@ -200,7 +226,7 @@
     ]
     for fetch in fetches:
         fetch.start()
-    pl.semaphore_wait(barrier, n + m - 2)
+    pl.semaphore_wait(barrier, n - 1 + flat * (m - 1))
 
     def block(index, k):
         return jac_ref.at[:, pl.ds(pl.multiple_of(index * width + k * span, span), span)]
@@ -225,7 +251,8 @@
 
     for fetch in fetches:
         fetch.wait()
-    walker_energies(elec, atom, quad, rotation, channels, coef, expo, base, energies)
+    share = -(-rows // m)
+    walker_energies(share, my_col * share, elec, atom, quad, rotation, channels, coef, expo, base, energies)
     cent_ref[...] = jnp.zeros_like(cent_ref)
     cent_ref[0, rows : rows + 1, :] = prev[...]
 
@@ -247,60 +274,72 @@
             preferred_element_type=jnp.float32,
         )
         gram = piece if gram is None else gram + piece
-    part[...] = gram.reshape(part.shape)
-
-    for s in order:
-        send(part.at[lax.rem(me + s, n)], shares, rs_send, rs_recv, s)
-    shares[me] = part[me]
-    wait_bytes(shares.at[pl.ds(0, n - 1)], rs_recv)
+    part[...] = (gram * scale).reshape(part.shape)
+    lane = lax.broadcasted_iota(jnp.int32, part.shape[1:], 1)
+    spare = jnp.broadcast_to(energies[:, 0:1], part.shape[1:])
+    part[me] = jnp.where(lane == rows + 1, spare, part[me])
+
+    def peer(s, t):
+        return lax.rem(inner + s, flat), lax.rem(my_col + t, m)
+
+    def send_plane(src, dst, send_sem, recv_sem, s, t):
+        there, core = peer(s, t)
+        pltpu.make_async_remote_copy(
+            src_ref=src,
+            dst_ref=dst,
+            send_sem=send_sem,
+            recv_sem=recv_sem,
+            device_id=(layer * flat + there, core),
+            device_id_type=MESH,
+        ).start()
+
+    others = [(s, t) for s in reversed(range(flat)) for t in range(m) if (s, t) != (0, 0)]
+    for s, t in others:
+        there, core = peer(s, t)
+        src = part.at[pl.ds((there * m + core) * groups, groups)]
+        send_plane(src, shares.at[rank], rs_send, rs_recv, s, t)
+    shares[rank] = part[own]
+    wait_bytes(shares.at[pl.ds(0, plane - 1)], rs_recv)
     acc = shares[0]
-    for i in range(1, n):
+    for i in range(1, plane):
         acc = acc + shares[i]
-    pair[my_col] = acc
-
-    def pair_copy(s, origin):
-        return pltpu.make_async_remote_copy(
-            src_ref=pair.at[my_col],
-            dst_ref=pair.at[origin],
-            send_sem=pair_send.at[s],
-            recv_sem=pair_recv.at[origin],
-            device_id=(me, lax.rem(my_col + s, m)),
+    layers = n // flat
+    lines[layer] = acc
+    for s in range(1, layers):
+        pltpu.make_async_remote_copy(
+            src_ref=lines.at[layer],
+            dst_ref=lines.at[layer],
+            send_sem=line_send,
+            recv_sem=line_recv,
+            device_id=(lax.rem(layer + s, layers) * flat + inner, my_col),
             device_id_type=MESH,
-        )
-
-    for s in range(1, m):
-        pair_copy(s, my_col).start()
-    for s in range(1, m):
-        pair_copy(s, lax.rem(my_col + s, m)).wait_recv()
-    acc = pair[0]
-    for c in range(1, m):
-        acc = acc + pair[c]
-    lane = lax.broadcasted_iota(jnp.int32, acc.shape, 1)
-    spare = jnp.broadcast_to(energies[:, 0:1], acc.shape)
-    full[me] = jnp.where(lane == rows + 1, spare, acc * scale)
-
-    for s in order:
-        send(full.at[me], full, ag_send, ag_recv, s)
-    wait_bytes(full.at[pl.ds(0, n - 1)], ag_recv)
+        ).start()
+    wait_bytes(lines.at[pl.ds(0, layers - 1)], line_recv)
+    acc = lines[0]
+    for i in range(1, layers):
+        acc = acc + lines[i]
+    full[own] = acc
+    for s, t in others:
+        send_plane(full.at[own], full.at[own], ag_send, ag_recv, s, t)
+    wait_bytes(full.at[pl.ds(0, (plane - 1) * groups)], ag_recv)
     if finish:
-        solve(n, rows, full, cent_ref, prev, energies, result_ref, energy_ref)
+        solve(n, rows, full, cent_ref, prev, spread_energy(full, me, rows), result_ref, energy_ref)
     else:
         result_ref[...] = full[...]
-        energy_ref[...] = jnp.broadcast_to(energies[0:rows, 0:1], (rows, 128))
+        energy_ref[...] = spread_energy(full, me, rows)
 
     for k in range(chunks):
         wait_bytes(cols.at[k, pl.ds(0, n - 1)], jac_send.at[k])
-    wait_bytes(part.at[pl.ds(0, n - 1)], rs_send)
-    wait_bytes(full.at[pl.ds(0, n - 1)], ag_send)
-    for s in range(1, m):
-        pair_copy(s, my_col).wait_send()
+    wait_bytes(shares.at[pl.ds(0, plane - 1)], rs_send)
+    wait_bytes(lines.at[pl.ds(0, layers - 1)], line_send)
+    wait_bytes(full.at[pl.ds(0, (plane - 1) * groups)], ag_send)
 
 
 def solve(n, rows, gram_ref, cent_ref, prev_ref, energy_ref, out_ref, mine_ref):
     index = lax.broadcasted_iota(jnp.int32, (rows, rows), 0)
     other = lax.broadcasted_iota(jnp.int32, (rows, rows), 1)
     mine_ref[...] = jnp.sum(
-        jnp.where(index == other, energy_ref[0:rows, 0:rows], 0.0), axis=0, keepdims=True
+        jnp.where(index == other, energy_ref[:, 0:rows], 0.0), axis=0, keepdims=True
     )
     wide = n * PAD
     walkers = n * rows
@@ -370,6 +409,7 @@
     dma = pltpu.SemaphoreType.DMA
     small = (prev_update, base, elec_pos, atom_pos, quad, rotation, channels, coef, expo)
     finish = wide <= 128
+    flat = plane_of(n, m)
     gram = (n, PAD, wide)
     cent = (n, PAD, width)
     scratch = [pltpu.VMEM(x.shape, x.dtype) for x in small]
@@ -387,14 +427,13 @@
         + [
             pltpu.VMEM((CHUNKS, n, rows, width // CHUNKS), f32),
             pltpu.VMEM(gram, f32),
-            pltpu.VMEM(gram, f32),
-            pltpu.VMEM((m, PAD, wide), f32),
+            pltpu.VMEM((flat * m, n // (flat * m), PAD, wide), f32),
+            pltpu.VMEM((n // flat, n // (flat * m), PAD, wide), f32),
             pltpu.VMEM(gram, f32),
             pltpu.VMEM((PAD, 128), f32),
         ]
-        + [dma((len(small),)), dma((CHUNKS,)), dma((CHUNKS,)), dma, dma]
-        + [dma((m,))] * 2
-        + [dma] * 2,
+        + [dma((len(small),)), dma((CHUNKS,)), dma((CHUNKS,))]
+        + [dma] * 6,
         compiler_params=pltpu.CompilerParams(collective_id=0, has_side_effects=True, vmem_limit_bytes=60 * 1024 * 1024),
     )(jacobian, *small)
 

time: 35.8 us -> 37 us (1.034)
  Pallas kernels: 33.2 us -> 34.4 us
    pallas_call x1, Pallas kernels: 33.2 us -> 34.4 us  [step(): pl.pallas_call(functools.partial(step_kernel, n, m, finish), out_shape=[j...]
where the time goes in v4:
time: 37 us; the launch traced here: 36.8 us
  Pallas kernels  34.4 us (93%)
  local copies, waits for them, and re-layouts  1.74 us (5%)
  between operations  0.66 us (2%)
    pallas_call x1, Pallas kernels, step(): pl.pallas_call(functools.partial(step_kernel, n, m, finish), out_shape=[j...  34.4 us
    unnamed x6, local copies, waits for them, and re-layouts  1.74 us

profile of v4, /device:TPU:0, one launch (start us, length us, event | category | flops | bytes accessed | tf_op | source)
XLA Modules:
  0.0 36.8 jit_solution(4706333164895081478)
XLA Ops:
  0.6 34.4 %shard_map.113 = (f32[1,6]{1,0:T(1,128)}, f32[1,1024]{1,0:T(1,128)}) custom-call(f32[6,16384]{1,0:T(8,128)} %jac_ref.1, f32[1,1024]{1,0:T(1,128)} %prev_ref.1, f32[1,6]{1,0:T(1,128)} %bitcast.9, f32[6,3,66]{2,1,0:T(4,128)} %elec_ref.1, f32[3,21]{1,0:T(4,128)} %atom_ref.1, f32[6,12,21,66]{3,2,1,0:T(8,128)} %bitcast.6, s32[6,66]{1,0:T(8,128)} %rotation_ref.1, ...), custom_call_target="tpu_custom_call" | custom-call | tf_op jit(solution)/shard_map/pallas_call | solution.py:421
  35.1 0.0 copy-start
  35.1 0.0 copy-start.1
  35.1 0.6 %copy-done.1 = f32[1,6]{1,0:T(1,128)S(1)} copy-done((f32[1,6]{1,0:T(1,128)S(1)}, f32[1,6]{1,0:T(1,128)}, u32[]{:S(2)}) %copy-start.1) | copy-done | bytes 48
  35.7 0.5 %copy.14 = f32[6]{0:T(128)} copy(f32[6]{0:T(128)S(1)} %bitcast.11) | data formatting | bytes 48
  36.2 0.0 copy-done
  36.2 0.6 %copy.15 = f32[1,1024]{1,0:T(1,128)} copy(f32[1,1024]{1,0:T(1,128)S(1)} %copy-done) | data formatting | bytes 8192
Async XLA Ops:
  35.1 1.2 %copy-start = (f32[1,1024]{1,0:T(1,128)S(1)}, f32[1,1024]{1,0:T(1,128)}, u32[]{:S(2)}) copy-start(f32[1,1024]{1,0:T(1,128)} %get-tuple-element.9) | copy-start | bytes 12292
  35.1 0.6 %copy-start.1 = (f32[1,6]{1,0:T(1,128)S(1)}, f32[1,6]{1,0:T(1,128)}, u32[]{:S(2)}) copy-start(f32[1,6]{1,0:T(1,128)} %get-tuple-element.4) | copy-start | bytes 76

commit v5 on v4

--- a/solution.py
+++ b/solution.py
@@ -17,7 +17,6 @@
 
 MESH = pl.DeviceIdType.MESH
 PAD = 8
-CHUNKS = 2
 
 
 def icosa_points():
@@ -119,14 +118,6 @@
     out[0:rows, :] = jnp.where(mine, out[0:rows, :] + first, 0.0)
 
 
-def far_first(n):
-    order, span = [], n
-    while span > 1:
-        order += [s for s in range(span // 2, n, span)]
-        span //= 2
-    return order + [s for s in range(1, n) if s not in order]
-
-
 def plane_of(n, m):
     flat = 4 if n % 4 == 0 else 1
     while n % (flat * m) != 0:
@@ -138,41 +129,27 @@
     return jnp.broadcast_to(full[me][0:rows, rows + 1 : rows + 2], (rows, 128))
 
 
+def energy_kernel(m, elec, atom, quad, rotation, channels, coef, expo, base, energies):
+    rows = quad.shape[0]
+    share = -(-rows // m)
+    begin = lax.axis_index("col") * share
+    walker_energies(share, begin, elec, atom, quad, rotation, channels, coef, expo, base, energies)
+
+
 def step_kernel(
     n,
     m,
     finish,
-    jac_ref,
-    prev_ref,
-    base_ref,
-    elec_ref,
-    atom_ref,
-    quad_ref,
-    rotation_ref,
-    channels_ref,
-    coef_ref,
-    expo_ref,
+    cols,
+    energies,
+    prev,
     energy_ref,
     result_ref,
     cent_ref,
-    prev,
-    base,
-    elec,
-    atom,
-    quad,
-    rotation,
-    channels,
-    coef,
-    expo,
-    cols,
     part,
     shares,
     lines,
     full,
-    energies,
-    fetch_sem,
-    jac_send,
-    jac_recv,
     rs_send,
     rs_recv,
     line_send,
@@ -182,11 +159,9 @@
 ):
     me = lax.axis_index("walk")
     my_col = lax.axis_index("col")
-    chunks, _, rows, span = cols.shape
-    width = chunks * span
+    _, rows, width = cols.shape
     walkers = rows * n
     scale = 1.0 / (width * n * m)
-    order = far_first(n)
     flat = plane_of(n, m)
     plane = flat * m
     groups = n // plane
@@ -196,84 +171,37 @@
     own = pl.ds(rank * groups, groups)
 
     barrier = pltpu.get_barrier_semaphore()
-    for s in order:
+    layers = n // flat
+    others = [(s, t) for s in reversed(range(flat)) for t in range(m) if (s, t) != (0, 0)]
+    for s, t in others:
+        there, core = lax.rem(inner + s, flat), lax.rem(my_col + t, m)
         pl.semaphore_signal(
-            barrier, inc=1, device_id=(lax.rem(me + s, n), my_col), device_id_type=MESH
+            barrier, inc=1, device_id=(layer * flat + there, core), device_id_type=MESH
         )
-    for s in range(flat):
-        for t in range(1, m):
-            pl.semaphore_signal(
-                barrier,
-                inc=1,
-                device_id=(layer * flat + lax.rem(inner + s, flat), lax.rem(my_col + t, m)),
-                device_id_type=MESH,
-            )
-    sources = (
-        quad_ref,
-        prev_ref,
-        base_ref,
-        elec_ref,
-        atom_ref,
-        rotation_ref,
-        channels_ref,
-        coef_ref,
-        expo_ref,
-    )
-    targets = (quad, prev, base, elec, atom, rotation, channels, coef, expo)
-    fetches = [
-        pltpu.make_async_copy(source, target, fetch_sem.at[k])
-        for k, (source, target) in enumerate(zip(sources, targets))
-    ]
-    for fetch in fetches:
-        fetch.start()
-    pl.semaphore_wait(barrier, n - 1 + flat * (m - 1))
-
-    def block(index, k):
-        return jac_ref.at[:, pl.ds(pl.multiple_of(index * width + k * span, span), span)]
-
-    def send(src, dst, send_sem, recv_sem, s):
-        pltpu.make_async_remote_copy(
-            src_ref=src,
-            dst_ref=dst.at[me],
-            send_sem=send_sem,
-            recv_sem=recv_sem,
-            device_id=(lax.rem(me + s, n), my_col),
-            device_id_type=MESH,
-        ).start()
+    for s in range(1, layers):
+        there = lax.rem(layer + s, layers) * flat + inner
+        pl.semaphore_signal(barrier, inc=1, device_id=(there, my_col), device_id_type=MESH)
 
     def wait_bytes(like, sem):
         pltpu.make_async_copy(like, like, sem).wait()
 
-    for k in range(chunks):
-        for s in order:
-            send(block(lax.rem(me + s, n), k), cols.at[k], jac_send.at[k], jac_recv.at[k], s)
-        pltpu.make_async_copy(block(me, k), cols.at[k, me], jac_recv.at[k]).start()
-
-    for fetch in fetches:
-        fetch.wait()
-    share = -(-rows // m)
-    walker_energies(share, my_col * share, elec, atom, quad, rotation, channels, coef, expo, base, energies)
     cent_ref[...] = jnp.zeros_like(cent_ref)
     cent_ref[0, rows : rows + 1, :] = prev[...]
 
-    gram = None
-    for k in range(chunks):
-        wait_bytes(cols.at[k], jac_recv.at[k])
-        total = cols[k, 0]
-        for i in range(1, n):
-            total = total + cols[k, i]
-        mean = jnp.sum(total, axis=0, keepdims=True) * (1.0 / walkers)
-        for i in range(n):
-            cent_ref[i, 0:rows, k * span : (k + 1) * span] = cols[k, i] - mean
-        cent = cent_ref[:, :, k * span : (k + 1) * span].reshape(n * PAD, span)
-        piece = lax.dot_general(
-            cent,
-            cent,
-            (((1,), (1,)), ((), ())),
-            precision=lax.Precision.HIGHEST,
-            preferred_element_type=jnp.float32,
-        )
-        gram = piece if gram is None else gram + piece
+    total = cols[0]
+    for i in range(1, n):
+        total = total + cols[i]
+    mean = jnp.sum(total, axis=0, keepdims=True) * (1.0 / walkers)
+    for i in range(n):
+        cent_ref[i, 0:rows, :] = cols[i] - mean
+    cent = cent_ref[...].reshape(n * PAD, width)
+    gram = lax.dot_general(
+        cent,
+        cent,
+        (((1,), (1,)), ((), ())),
+        precision=lax.Precision.HIGHEST,
+        preferred_element_type=jnp.float32,
+    )
     part[...] = (gram * scale).reshape(part.shape)
     lane = lax.broadcasted_iota(jnp.int32, part.shape[1:], 1)
     spare = jnp.broadcast_to(energies[:, 0:1], part.shape[1:])
@@ -293,7 +221,7 @@
             device_id_type=MESH,
         ).start()
 
-    others = [(s, t) for s in reversed(range(flat)) for t in range(m) if (s, t) != (0, 0)]
+    pl.semaphore_wait(barrier, len(others) + layers - 1)
     for s, t in others:
         there, core = peer(s, t)
         src = part.at[pl.ds((there * m + core) * groups, groups)]
@@ -303,7 +231,6 @@
     acc = shares[0]
     for i in range(1, plane):
         acc = acc + shares[i]
-    layers = n // flat
     lines[layer] = acc
     for s in range(1, layers):
         pltpu.make_async_remote_copy(
@@ -328,8 +255,6 @@
         result_ref[...] = full[...]
         energy_ref[...] = spread_energy(full, me, rows)
 
-    for k in range(chunks):
-        wait_bytes(cols.at[k, pl.ds(0, n - 1)], jac_send.at[k])
     wait_bytes(shares.at[pl.ds(0, plane - 1)], rs_send)
     wait_bytes(lines.at[pl.ds(0, layers - 1)], line_send)
     wait_bytes(full.at[pl.ds(0, (plane - 1) * groups)], ag_send)
@@ -399,43 +324,49 @@
     out_ref[...] = jnp.sum(acc, axis=0, keepdims=True) + momentum * prev_ref[...]
 
 
-def step(n, m, jacobian, prev_update, base, elec_pos, atom_pos, quad, rotation, channels, coef, expo):
-    rows = jacobian.shape[0]
-    width = jacobian.shape[1] // n
+def walkers_mine(m, elec_pos, atom_pos, quad, rotation, channels, coef, expo, base):
+    return pl.pallas_call(
+        functools.partial(energy_kernel, m),
+        out_shape=jax.ShapeDtypeStruct((PAD, 128), jnp.float32),
+        compiler_params=pltpu.CompilerParams(vmem_limit_bytes=32 * 1024 * 1024),
+        cost_estimate=pl.CostEstimate(
+            flops=30 * quad.size, bytes_accessed=4 * quad.size, transcendentals=quad.size
+        ),
+    )(elec_pos, atom_pos, quad, rotation, channels, coef, expo, base)
+
+
+def step(n, m, cols, energies, prev_update):
+    _, rows, width = cols.shape
     wide = n * PAD
     vmem = pl.BlockSpec(memory_space=pltpu.VMEM)
-    hbm = pl.BlockSpec(memory_space=pltpu.HBM)
     f32 = jnp.float32
-    dma = pltpu.SemaphoreType.DMA
-    small = (prev_update, base, elec_pos, atom_pos, quad, rotation, channels, coef, expo)
     finish = wide <= 128
     flat = plane_of(n, m)
     gram = (n, PAD, wide)
     cent = (n, PAD, width)
-    scratch = [pltpu.VMEM(x.shape, x.dtype) for x in small]
     if finish:
         shapes = [(1, rows), prev_update.shape]
-        scratch = [pltpu.VMEM(cent, f32)] + scratch
+        scratch = [pltpu.VMEM(cent, f32)]
     else:
         shapes = [(rows, 128), gram, cent]
+        scratch = []
     return pl.pallas_call(
         functools.partial(step_kernel, n, m, finish),
         out_shape=[jax.ShapeDtypeStruct(shape, f32) for shape in shapes],
-        in_specs=[hbm] * 10,
+        in_specs=[vmem] * 3,
         out_specs=[vmem] * len(shapes),
         scratch_shapes=scratch
         + [
-            pltpu.VMEM((CHUNKS, n, rows, width // CHUNKS), f32),
             pltpu.VMEM(gram, f32),
             pltpu.VMEM((flat * m, n // (flat * m), PAD, wide), f32),
             pltpu.VMEM((n // flat, n // (flat * m), PAD, wide), f32),
             pltpu.VMEM(gram, f32),
-            pltpu.VMEM((PAD, 128), f32),
         ]
-        + [dma((len(small),)), dma((CHUNKS,)), dma((CHUNKS,))]
-        + [dma] * 6,
-        compiler_params=pltpu.CompilerParams(collective_id=0, has_side_effects=True, vmem_limit_bytes=60 * 1024 * 1024),
-    )(jacobian, *small)
+        + [pltpu.SemaphoreType.DMA] * 6,
+        compiler_params=pltpu.CompilerParams(
+            collective_id=0, has_side_effects=True, vmem_limit_bytes=32 * 1024 * 1024
+        ),
+    )(cols, energies, prev_update)
 
 
 def finish_outside(n, rows, gram, cent, prev_update):
@@ -469,12 +400,10 @@
     ecp_expo,
 ):
     rows = jacobian.shape[0]
-    energy, result, *cent = step(
-        n,
+    split = jacobian.reshape(rows, n, -1)
+    cols = lax.all_to_all(split, "walk", split_axis=1, concat_axis=0, tiled=False)
+    energies = walkers_mine(
         m,
-        jacobian,
-        prev_update,
-        base_energy.reshape(1, -1),
         elec_pos,
         atom_pos,
         jnp.transpose(quad_ratio, (0, 3, 1, 2)),
@@ -482,7 +411,9 @@
         channels.reshape(1, -1),
         ecp_coef.T,
         ecp_expo.T,
+        base_energy.reshape(1, -1),
     )
+    energy, result, *cent = step(n, m, cols, energies, prev_update)
     if cent:
         return (energy[:, 0], finish_outside(n, rows, result, cent[0], prev_update))
     return (energy.reshape(rows), result)

time: 37 us -> 41.5 us (1.12)
  Pallas kernels: 34.4 us -> 16.1 us
  waiting for transfers between devices: 0 us -> 10.8 us
  starting transfers between devices: 0 us -> 8.44 us
  local copies, waits for them, and re-layouts: 1.74 us -> 4.98 us
    pallas_call x1, Pallas kernels: 34.4 us -> 15 us  [step(): pl.pallas_call(functools.partial(step_kernel, n, m, finish), out_shape=[j...]
    all_to_all x0 -> x1, waiting for transfers between devices: none -> 10.8 us  [body(): lax.all_to_all(split, 'walk', split_axis=1, concat_axis=0, tiled=False)]
    all_to_all x0 -> x1, starting transfers between devices: none -> 8.44 us  [body(): lax.all_to_all(split, 'walk', split_axis=1, concat_axis=0, tiled=False)]
    unnamed x6 -> x21, local copies, waits for them, and re-layouts: 1.74 us -> 3.46 us
    another operation x0 -> x1, local copies, waits for them, and re-layouts: none -> 1.15 us  [body(): lax.all_to_all(split, 'walk', split_axis=1, concat_axis=0, tiled=False)]
    pallas_call x0 -> x1, Pallas kernels: none -> 1.08 us  [walkers_mine(): pl.pallas_call(functools.partial(energy_kernel, m), out_shape=jax.ShapeDt...]
  transfers between devices with their start and end apart: 0 -> 1, of which waited for: 0 -> 1; matrix products, arithmetic and copies ran while one was open for 0% -> 0% of each run, Pallas kernels for 0% -> 3%
where the time goes in v5:
time: 41.5 us; the launch traced here: 41.1 us
  Pallas kernels  16.1 us (39%)
  waiting for transfers between devices  10.8 us (26%)
  starting transfers between devices  8.44 us (20%)
  local copies, waits for them, and re-layouts  4.98 us (12%)
  between operations  0.74 us (2%)
    pallas_call x1, Pallas kernels, step(): pl.pallas_call(functools.partial(step_kernel, n, m, finish), out_shape=[j...  15 us
    all_to_all x1, waiting for transfers between devices, body(): lax.all_to_all(split, 'walk', split_axis=1, concat_axis=0, tiled=False)  10.8 us
    all_to_all x1, starting transfers between devices, body(): lax.all_to_all(split, 'walk', split_axis=1, concat_axis=0, tiled=False)  8.44 us
    unnamed x21, local copies, waits for them, and re-layouts  3.46 us
    another operation x1, local copies, waits for them, and re-layouts, body(): lax.all_to_all(split, 'walk', split_axis=1, concat_axis=0, tiled=False)  1.15 us
    pallas_call x1, Pallas kernels, walkers_mine(): pl.pallas_call(functools.partial(energy_kernel, m), out_shape=jax.ShapeDt...  1.08 us
  transfers between devices with their start and end apart: 1, of which 1 were waited for; matrix products, arithmetic and copies ran while one was open for 0% of the time, Pallas kernels for 3%

profile of v5, /device:TPU:0, one launch (start us, length us, event | category | flops | bytes accessed | tf_op | source)
XLA Modules:
  0.0 41.1 jit_solution(336922783717495895)
XLA Ops:
  0.6 1.3 %copy.20 = f32[1,6,16,1024]{3,2,1,0:T(8,128)S(1)} copy(f32[1,6,16,1024]{3,1,2,0:T(8,128)} %bitcast.27) | data formatting | bytes 786432
  1.9 0.0 copy-start
  1.9 1.1 %copy.12 = f32[1,6,16,1024]{3,0,1,2:T(1,128)} copy(f32[1,6,16,1024]{3,2,1,0:T(8,128)S(1)} %copy.20) | data formatting | bytes 786432 | tf_op jit(solution)/shard_map/broadcast_in_dim;reshape | solution.py:404
  3.1 8.4 %all-to-all-start = ((f32[1,6,16,1024]{3,0,1,2:T(1,128)}), f32[1,6,16,1024]{3,0,1,2:T(1,128)S(1)}, u32[]{:S(2)}, u32[]{:S(2)}) async-start(f32[1,6,16,1024]{3,0,1,2:T(1,128)} %copy.12), calls=%async_computation | async-start | bytes 786432 | tf_op jit(solution)/shard_map/all_to_all | solution.py:404
  11.5 0.0 copy-start.2
  11.5 0.0 copy-start.4
  11.5 0.0 copy-start.7
  11.6 0.0 copy-start.8
  11.6 0.0 copy-done
  11.6 0.0 copy-done.1
  11.6 0.0 copy-done.5
  11.6 0.0 copy-done.6
  11.6 0.6 %copy-done.2 = s32[6,66]{1,0:T(8,128)S(1)} copy-done((s32[6,66]{1,0:T(8,128)S(1)}, s32[6,66]{1,0:T(8,128)}, u32[]{:S(2)}) %copy-start.2) | copy-done | bytes 1608
  12.2 0.0 copy-done.4
  12.2 0.0 copy-done.7
  12.2 1.1 %shard_map.113.energies = f32[8,128]{1,0:T(8,128)S(1)} custom-call(f32[6,3,66]{2,1,0:T(4,128)S(1)} %copy-done.1, f32[3,21]{1,0:T(4,128)S(1)} %copy-done.4, f32[6,12,21,66]{3,2,1,0:T(8,128)S(1)} %bitcast.20, s32[6,66]{1,0:T(8,128)S(1)} %copy-done.2, s32[1,21]{1,0:T(1,128)S(1)} %bitcast.23, f32[3,21]{1,0:T(4,128)S(1)} %bitcast.21, f32[3,21]{1,0:T(4,128)S(1)} %bitcast.22, ...), custom_call_target="tpu_custom_call" | custom-call | flops 2993760 | bytes 399168 | tf_op jit(solution)/shard_map/pallas_call | solution.py:328
  13.3 10.8 %all-to-all-done = f32[1,6,16,1024]{3,0,1,2:T(1,128)S(1)} async-done(((f32[1,6,16,1024]{3,0,1,2:T(1,128)}), f32[1,6,16,1024]{3,0,1,2:T(1,128)S(1)}, u32[]{:S(2)}, u32[]{:S(2)}) %all-to-all-start) | async-done | bytes 393248 | tf_op jit(solution)/shard_map/all_to_all | solution.py:404
  24.2 0.1 copy.21
  24.3 0.0 copy-start.3
  24.3 0.2 copy.19
  24.6 0.4 %copy-done.3 = f32[1,1024]{1,0:T(1,128)S(1)} copy-done((f32[1,1024]{1,0:T(1,128)S(1)}, f32[1,1024]{1,0:T(1,128)}, u32[]{:S(2)}) %copy-start.3) | copy-done | bytes 4120
  25.0 15.0 %shard_map.114 = (f32[1,6]{1,0:T(1,128)S(1)}, f32[1,1024]{1,0:T(1,128)S(1)}) custom-call(f32[16,6,1024]{2,1,0:T(8,128)S(1)} %bitcast.19, f32[8,128]{1,0:T(8,128)S(1)} %shard_map.113.energies, f32[1,1024]{1,0:T(1,128)S(1)} %copy-done.3), custom_call_target="tpu_custom_call" | custom-call | tf_op jit(solution)/shard_map/pallas_call | solution.py:353
  40.0 0.5 %copy.24 = f32[6]{0:T(128)} copy(f32[6]{0:T(128)S(1)} %bitcast.25) | data formatting | bytes 48
  40.5 0.6 %copy.25 = f32[1,1024]{1,0:T(1,128)} copy(f32[1,1024]{1,0:T(1,128)S(1)} %get-tuple-element.9) | data formatting | bytes 8192
  (4 shorter events, 0.0 us)
Async XLA Ops:
  1.9 9.7 %copy-start = (f32[6,21,66,12]{2,1,3,0:T(8,128)S(1)}, f32[6,21,66,12]{2,1,3,0:T(8,128)}, u32[]{:S(2)}) copy-start(f32[6,21,66,12]{2,1,3,0:T(8,128)} %param.15) | copy-start | bytes 1197508
  3.1 8.5 %copy-start.1 = (f32[6,3,66]{2,1,0:T(4,128)S(1)}, f32[6,3,66]{2,1,0:T(4,128)}, u32[]{:S(2)}) copy-start(f32[6,3,66]{2,1,0:T(4,128)} %elec.1) | copy-start | bytes 14260
  3.1 8.5 %copy-start.5 = (f32[21,3]{0,1:T(4,128)S(1)}, f32[21,3]{0,1:T(4,128)}, u32[]{:S(2)}) copy-start(f32[21,3]{0,1:T(4,128)} %param.18) | copy-start | bytes 760
  3.1 8.5 %copy-start.6 = (f32[21,3]{0,1:T(4,128)S(1)}, f32[21,3]{0,1:T(4,128)}, u32[]{:S(2)}) copy-start(f32[21,3]{0,1:T(4,128)} %param.19) | copy-start | bytes 760
  3.1 21.1 %all-to-all-start = ((f32[1,6,16,1024]{3,0,1,2:T(1,128)}), f32[1,6,16,1024]{3,0,1,2:T(1,128)S(1)}, u32[]{:S(2)}, u32[]{:S(2)}) async-start(f32[1,6,16,1024]{3,0,1,2:T(1,128)} %copy.12), calls=%async_computation | async-start | bytes 786432 | tf_op jit(solution)/shard_map/all_to_all | solution.py:404
  11.5 0.7 %copy-start.2 = (s32[6,66]{1,0:T(8,128)S(1)}, s32[6,66]{1,0:T(8,128)}, u32[]{:S(2)}) copy-start(s32[6,66]{1,0:T(8,128)} %rotation.1) | copy-start | bytes 4756
  11.5 0.7 %copy-start.4 = (f32[3,21]{1,0:T(4,128)S(1)}, f32[3,21]{1,0:T(4,128)}, u32[]{:S(2)}) copy-start(f32[3,21]{1,0:T(4,128)} %atom.1) | copy-start | bytes 760
  11.5 0.7 %copy-start.7 = (s32[21]{0:T(128)S(1)}, s32[21]{0:T(128)}, u32[]{:S(2)}) copy-start(s32[21]{0:T(128)} %param.17) | copy-start | bytes 256
  11.6 0.7 %copy-start.8 = (f32[6]{0:T(128)S(1)}, f32[6]{0:T(128)}, u32[]{:S(2)}) copy-start(f32[6]{0:T(128)} %param.12) | copy-start | bytes 76
  24.3 0.7 %copy-start.3 = (f32[1,1024]{1,0:T(1,128)S(1)}, f32[1,1024]{1,0:T(1,128)}, u32[]{:S(2)}) copy-start(f32[1,1024]{1,0:T(1,128)} %prev.1) | copy-start | bytes 12292

commit v6 on v4

--- a/solution.py
+++ b/solution.py
@@ -127,11 +127,17 @@
     return order + [s for s in range(1, n) if s not in order]
 
 
-def plane_of(n, m):
-    flat = 4 if n % 4 == 0 else 1
-    while n % (flat * m) != 0:
-        flat -= 1
-    return flat
+def each(count, act):
+    if count <= 64:
+        for s in far_first(count):
+            act(s)
+        return
+
+    def turn(s, _):
+        act(s)
+        return 0
+
+    lax.fori_loop(1, count, turn, 0)
 
 
 def spread_energy(full, me, rows):
@@ -167,7 +173,6 @@
     cols,
     part,
     shares,
-    lines,
     full,
     energies,
     fetch_sem,
@@ -175,8 +180,6 @@
     jac_recv,
     rs_send,
     rs_recv,
-    line_send,
-    line_recv,
     ag_send,
     ag_recv,
 ):
@@ -187,27 +190,18 @@
     walkers = rows * n
     scale = 1.0 / (width * n * m)
     order = far_first(n)
-    flat = plane_of(n, m)
-    plane = flat * m
-    groups = n // plane
-    layer = me // flat
-    inner = lax.rem(me, flat)
-    rank = inner * m + my_col
-    own = pl.ds(rank * groups, groups)
-
     barrier = pltpu.get_barrier_semaphore()
-    for s in order:
-        pl.semaphore_signal(
-            barrier, inc=1, device_id=(lax.rem(me + s, n), my_col), device_id_type=MESH
-        )
-    for s in range(flat):
-        for t in range(1, m):
-            pl.semaphore_signal(
-                barrier,
-                inc=1,
-                device_id=(layer * flat + lax.rem(inner + s, flat), lax.rem(my_col + t, m)),
-                device_id_type=MESH,
-            )
+    mine = me * m + my_col
+    owner = lax.rem(me, m) == my_col
+
+    def device(s):
+        place = lax.rem(mine + s, n * m)
+        return place // m, lax.rem(place, m)
+
+    def greet(s):
+        pl.semaphore_signal(barrier, inc=1, device_id=device(s), device_id_type=MESH)
+
+    each(n * m, greet)
     sources = (
         quad_ref,
         prev_ref,
@@ -226,7 +220,7 @@
     ]
     for fetch in fetches:
         fetch.start()
-    pl.semaphore_wait(barrier, n - 1 + flat * (m - 1))
+    pl.semaphore_wait(barrier, n * m - 1)
 
     def block(index, k):
         return jac_ref.at[:, pl.ds(pl.multiple_of(index * width + k * span, span), span)]
@@ -279,49 +273,47 @@
     spare = jnp.broadcast_to(energies[:, 0:1], part.shape[1:])
     part[me] = jnp.where(lane == rows + 1, spare, part[me])
 
-    def peer(s, t):
-        return lax.rem(inner + s, flat), lax.rem(my_col + t, m)
-
-    def send_plane(src, dst, send_sem, recv_sem, s, t):
-        there, core = peer(s, t)
+    def send_part(there):
         pltpu.make_async_remote_copy(
-            src_ref=src,
-            dst_ref=dst,
-            send_sem=send_sem,
-            recv_sem=recv_sem,
-            device_id=(layer * flat + there, core),
+            src_ref=part.at[there],
+            dst_ref=shares.at[mine],
+            send_sem=rs_send,
+            recv_sem=rs_recv,
+            device_id=(there, lax.rem(there, m)),
             device_id_type=MESH,
         ).start()
 
-    others = [(s, t) for s in reversed(range(flat)) for t in range(m) if (s, t) != (0, 0)]
-    for s, t in others:
-        there, core = peer(s, t)
-        src = part.at[pl.ds((there * m + core) * groups, groups)]
-        send_plane(src, shares.at[rank], rs_send, rs_recv, s, t)
-    shares[rank] = part[own]
-    wait_bytes(shares.at[pl.ds(0, plane - 1)], rs_recv)
-    acc = shares[0]
-    for i in range(1, plane):
-        acc = acc + shares[i]
-    layers = n // flat
-    lines[layer] = acc
-    for s in range(1, layers):
+    def send_sum(s):
         pltpu.make_async_remote_copy(
-            src_ref=lines.at[layer],
-            dst_ref=lines.at[layer],
-            send_sem=line_send,
-            recv_sem=line_recv,
-            device_id=(lax.rem(layer + s, layers) * flat + inner, my_col),
+            src_ref=full.at[me],
+            dst_ref=full.at[me],
+            send_sem=ag_send,
+            recv_sem=ag_recv,
+            device_id=device(s),
             device_id_type=MESH,
         ).start()
-    wait_bytes(lines.at[pl.ds(0, layers - 1)], line_recv)
-    acc = lines[0]
-    for i in range(1, layers):
-        acc = acc + lines[i]
-    full[own] = acc
-    for s, t in others:
-        send_plane(full.at[own], full.at[own], ag_send, ag_recv, s, t)
-    wait_bytes(full.at[pl.ds(0, (plane - 1) * groups)], ag_recv)
+
+    for s in order:
+        send_part(lax.rem(me + s, n))
+
+    @pl.when(jnp.logical_not(owner))
+    def _():
+        send_part(me)
+        wait_bytes(full, ag_recv)
+        wait_bytes(part, rs_send)
+
+    @pl.when(owner)
+    def _():
+        shares[mine] = part[me]
+        wait_bytes(shares.at[pl.ds(0, n * m - 1)], rs_recv)
+        sums = [shares[i] for i in range(n * m)]
+        while len(sums) > 1:
+            sums = [sum(sums[i : i + 2]) for i in range(0, len(sums), 2)]
+        full[me] = sums[0]
+        each(n * m, send_sum)
+        wait_bytes(full.at[pl.ds(0, n - 1)], ag_recv)
+        wait_bytes(part.at[pl.ds(0, n - 1)], rs_send)
+
     if finish:
         solve(n, rows, full, cent_ref, prev, spread_energy(full, me, rows), result_ref, energy_ref)
     else:
@@ -330,9 +322,9 @@
 
     for k in range(chunks):
         wait_bytes(cols.at[k, pl.ds(0, n - 1)], jac_send.at[k])
-    wait_bytes(shares.at[pl.ds(0, plane - 1)], rs_send)
-    wait_bytes(lines.at[pl.ds(0, layers - 1)], line_send)
-    wait_bytes(full.at[pl.ds(0, (plane - 1) * groups)], ag_send)
+    @pl.when(owner)
+    def _():
+        wait_bytes(shares.at[pl.ds(0, n * m - 1)], ag_send)
 
 
 def solve(n, rows, gram_ref, cent_ref, prev_ref, energy_ref, out_ref, mine_ref):
@@ -409,7 +401,6 @@
     dma = pltpu.SemaphoreType.DMA
     small = (prev_update, base, elec_pos, atom_pos, quad, rotation, channels, coef, expo)
     finish = wide <= 128
-    flat = plane_of(n, m)
     gram = (n, PAD, wide)
     cent = (n, PAD, width)
     scratch = [pltpu.VMEM(x.shape, x.dtype) for x in small]
@@ -427,13 +418,12 @@
         + [
             pltpu.VMEM((CHUNKS, n, rows, width // CHUNKS), f32),
             pltpu.VMEM(gram, f32),
-            pltpu.VMEM((flat * m, n // (flat * m), PAD, wide), f32),
-            pltpu.VMEM((n // flat, n // (flat * m), PAD, wide), f32),
+            pltpu.VMEM((n * m, PAD, wide), f32),
             pltpu.VMEM(gram, f32),
             pltpu.VMEM((PAD, 128), f32),
         ]
         + [dma((len(small),)), dma((CHUNKS,)), dma((CHUNKS,))]
-        + [dma] * 6,
+        + [dma] * 4,
         compiler_params=pltpu.CompilerParams(collective_id=0, has_side_effects=True, vmem_limit_bytes=60 * 1024 * 1024),
     )(jacobian, *small)
 

time: 37 us -> 36.2 us (0.978)
  Pallas kernels: 34.4 us -> 33.7 us
    pallas_call x1, Pallas kernels: 34.4 us -> 33.7 us  [step(): pl.pallas_call(functools.partial(step_kernel, n, m, finish), out_shape=[j...]
where the time goes in v6:
time: 36.2 us; the launch traced here: 36.1 us
  Pallas kernels  33.7 us (93%)
  local copies, waits for them, and re-layouts  1.74 us (5%)
  between operations  0.66 us (2%)
    pallas_call x1, Pallas kernels, step(): pl.pallas_call(functools.partial(step_kernel, n, m, finish), out_shape=[j...  33.7 us
    unnamed x6, local copies, waits for them, and re-layouts  1.74 us

profile of v6, /device:TPU:0, one launch (start us, length us, event | category | flops | bytes accessed | tf_op | source)
XLA Modules:
  0.0 36.1 jit_solution(15453909374476520365)
XLA Ops:
  0.6 33.7 %shard_map.113 = (f32[1,6]{1,0:T(1,128)}, f32[1,1024]{1,0:T(1,128)}) custom-call(f32[6,16384]{1,0:T(8,128)} %jac_ref.1, f32[1,1024]{1,0:T(1,128)} %prev_ref.1, f32[1,6]{1,0:T(1,128)} %bitcast.9, f32[6,3,66]{2,1,0:T(4,128)} %elec_ref.1, f32[3,21]{1,0:T(4,128)} %atom_ref.1, f32[6,12,21,66]{3,2,1,0:T(8,128)} %bitcast.6, s32[6,66]{1,0:T(8,128)} %rotation_ref.1, ...), custom_call_target="tpu_custom_call" | custom-call | tf_op jit(solution)/shard_map/pallas_call | solution.py:412
  34.3 0.0 copy-start
  34.3 0.0 copy-start.1
  34.3 0.6 %copy-done.1 = f32[1,6]{1,0:T(1,128)S(1)} copy-done((f32[1,6]{1,0:T(1,128)S(1)}, f32[1,6]{1,0:T(1,128)}, u32[]{:S(2)}) %copy-start.1) | copy-done | bytes 48
  35.0 0.5 %copy.14 = f32[6]{0:T(128)} copy(f32[6]{0:T(128)S(1)} %bitcast.11) | data formatting | bytes 48
  35.5 0.0 copy-done
  35.5 0.6 %copy.15 = f32[1,1024]{1,0:T(1,128)} copy(f32[1,1024]{1,0:T(1,128)S(1)} %copy-done) | data formatting | bytes 8192
Async XLA Ops:
  34.3 1.2 %copy-start = (f32[1,1024]{1,0:T(1,128)S(1)}, f32[1,1024]{1,0:T(1,128)}, u32[]{:S(2)}) copy-start(f32[1,1024]{1,0:T(1,128)} %get-tuple-element.9) | copy-start | bytes 12292
  34.3 0.6 %copy-start.1 = (f32[1,6]{1,0:T(1,128)S(1)}, f32[1,6]{1,0:T(1,128)}, u32[]{:S(2)}) copy-start(f32[1,6]{1,0:T(1,128)} %get-tuple-element.4) | copy-start | bytes 76

commit v7 on v3

--- a/solution.py
+++ b/solution.py
@@ -17,7 +17,7 @@
 
 MESH = pl.DeviceIdType.MESH
 PAD = 8
-CHUNKS = 2
+CHUNKS = 1
 
 
 def icosa_points():
@@ -151,12 +151,15 @@
     coef,
     expo,
     cols,
+    relay,
     part,
     shares,
     pair,
     full,
     energies,
     fetch_sem,
+    line_send,
+    line_recv,
     jac_send,
     jac_recv,
     rs_send,
@@ -173,6 +176,10 @@
     walkers = rows * n
     scale = 1.0 / (width * n * m)
     order = far_first(n)
+    layers = relay.shape[0]
+    flat = n // layers
+    layer = me // flat
+    inner = lax.rem(me, flat)
     barrier = pltpu.get_barrier_semaphore()
     for s in order:
         pl.semaphore_signal(
@@ -218,14 +225,44 @@
     def wait_bytes(like, sem):
         pltpu.make_async_copy(like, like, sem).wait()
 
-    for k in range(chunks):
-        for s in order:
-            send(block(lax.rem(me + s, n), k), cols.at[k], jac_send.at[k], jac_recv.at[k], s)
-        pltpu.make_async_copy(block(me, k), cols.at[k, me], jac_recv.at[k]).start()
+    for s in far_first(layers):
+        there = lax.rem(layer + s, layers)
+        bulk = flat * width
+        pltpu.make_async_remote_copy(
+            src_ref=jac_ref.at[:, pl.ds(pl.multiple_of(there * bulk, bulk), bulk)],
+            dst_ref=relay.at[layer],
+            send_sem=line_send,
+            recv_sem=line_recv.at[layer],
+            device_id=(there * flat + inner, my_col),
+            device_id_type=MESH,
+        ).start()
+
+    def hand_out(pick, origin):
+        for s in range(1, flat):
+            there = lax.rem(inner + s, flat)
+            pltpu.make_async_remote_copy(
+                src_ref=pick(there),
+                dst_ref=cols.at[0, origin],
+                send_sem=jac_send.at[0],
+                recv_sem=jac_recv.at[0],
+                device_id=(layer * flat + there, my_col),
+                device_id_type=MESH,
+            ).start()
+        pltpu.make_async_copy(pick(inner), cols.at[0, origin], jac_recv.at[0]).start()
+
+    hand_out(lambda there: block(layer * flat + there, 0), me)
 
     for fetch in fetches:
         fetch.wait()
     walker_energies(elec, atom, quad, rotation, channels, coef, expo, base, energies)
+    for s in far_first(layers):
+        origin = lax.rem(layer + layers - s, layers)
+        wait_bytes(relay.at[origin], line_recv.at[origin])
+
+        def pick(there):
+            return relay.at[origin, :, pl.ds(pl.multiple_of(there * width, width), width)]
+
+        hand_out(pick, origin * flat + inner)
     cent_ref[...] = jnp.zeros_like(cent_ref)
     cent_ref[0, rows : rows + 1, :] = prev[...]
 
@@ -289,7 +326,8 @@
         energy_ref[...] = jnp.broadcast_to(energies[0:rows, 0:1], (rows, 128))
 
     for k in range(chunks):
-        wait_bytes(cols.at[k, pl.ds(0, n - 1)], jac_send.at[k])
+        wait_bytes(cols.at[k, pl.ds(0, n - layers)], jac_send.at[k])
+    wait_bytes(relay.at[pl.ds(0, layers - 1)], line_send)
     wait_bytes(part.at[pl.ds(0, n - 1)], rs_send)
     wait_bytes(full.at[pl.ds(0, n - 1)], ag_send)
     for s in range(1, m):
@@ -370,6 +408,7 @@
     dma = pltpu.SemaphoreType.DMA
     small = (prev_update, base, elec_pos, atom_pos, quad, rotation, channels, coef, expo)
     finish = wide <= 128
+    flat = 4 if n % 4 == 0 else 1
     gram = (n, PAD, wide)
     cent = (n, PAD, width)
     scratch = [pltpu.VMEM(x.shape, x.dtype) for x in small]
@@ -386,13 +425,14 @@
         scratch_shapes=scratch
         + [
             pltpu.VMEM((CHUNKS, n, rows, width // CHUNKS), f32),
+            pltpu.VMEM((n // flat, rows, flat * width), f32),
             pltpu.VMEM(gram, f32),
             pltpu.VMEM(gram, f32),
             pltpu.VMEM((m, PAD, wide), f32),
             pltpu.VMEM(gram, f32),
             pltpu.VMEM((PAD, 128), f32),
         ]
-        + [dma((len(small),)), dma((CHUNKS,)), dma((CHUNKS,)), dma, dma]
+        + [dma((len(small),)), dma, dma((n // flat,)), dma((CHUNKS,)), dma((CHUNKS,)), dma, dma]
         + [dma((m,))] * 2
         + [dma] * 2,
         compiler_params=pltpu.CompilerParams(collective_id=0, has_side_effects=True, vmem_limit_bytes=60 * 1024 * 1024),

time: 35.8 us -> 39 us (1.089)
  Pallas kernels: 33.2 us -> 36.4 us
    pallas_call x1, Pallas kernels: 33.2 us -> 36.4 us  [step(): pl.pallas_call(functools.partial(step_kernel, n, m, finish), out_shape=[j...]
where the time goes in v7:
time: 39 us; the launch traced here: 38.8 us
  Pallas kernels  36.4 us (93%)
  local copies, waits for them, and re-layouts  1.74 us (4%)
  between operations  0.66 us (2%)
    pallas_call x1, Pallas kernels, step(): pl.pallas_call(functools.partial(step_kernel, n, m, finish), out_shape=[j...  36.4 us
    unnamed x6, local copies, waits for them, and re-layouts  1.74 us

profile of v7, /device:TPU:0, one launch (start us, length us, event | category | flops | bytes accessed | tf_op | source)
XLA Modules:
  0.0 38.8 jit_solution(2337616222578925828)
XLA Ops:
  0.6 36.4 %shard_map.113 = (f32[1,6]{1,0:T(1,128)}, f32[1,1024]{1,0:T(1,128)}) custom-call(f32[6,16384]{1,0:T(8,128)} %jac_ref.1, f32[1,1024]{1,0:T(1,128)} %prev_ref.1, f32[1,6]{1,0:T(1,128)} %bitcast.9, f32[6,3,66]{2,1,0:T(4,128)} %elec_ref.1, f32[3,21]{1,0:T(4,128)} %atom_ref.1, f32[6,12,21,66]{3,2,1,0:T(8,128)} %bitcast.6, s32[6,66]{1,0:T(8,128)} %rotation_ref.1, ...), custom_call_target="tpu_custom_call" | custom-call | tf_op jit(solution)/shard_map/pallas_call | solution.py:420
  37.1 0.0 copy-start
  37.1 0.0 copy-start.1
  37.1 0.6 %copy-done.1 = f32[1,6]{1,0:T(1,128)S(1)} copy-done((f32[1,6]{1,0:T(1,128)S(1)}, f32[1,6]{1,0:T(1,128)}, u32[]{:S(2)}) %copy-start.1) | copy-done | bytes 48
  37.7 0.5 %copy.14 = f32[6]{0:T(128)} copy(f32[6]{0:T(128)S(1)} %bitcast.11) | data formatting | bytes 48
  38.2 0.0 copy-done
  38.2 0.6 %copy.15 = f32[1,1024]{1,0:T(1,128)} copy(f32[1,1024]{1,0:T(1,128)S(1)} %copy-done) | data formatting | bytes 8192
Async XLA Ops:
  37.1 1.2 %copy-start = (f32[1,1024]{1,0:T(1,128)S(1)}, f32[1,1024]{1,0:T(1,128)}, u32[]{:S(2)}) copy-start(f32[1,1024]{1,0:T(1,128)} %get-tuple-element.9) | copy-start | bytes 12292
  37.1 0.6 %copy-start.1 = (f32[1,6]{1,0:T(1,128)S(1)}, f32[1,6]{1,0:T(1,128)}, u32[]{:S(2)}) copy-start(f32[1,6]{1,0:T(1,128)} %get-tuple-element.4) | copy-start | bytes 76

commit v8 on v3

--- a/solution.py
+++ b/solution.py
@@ -399,6 +399,19 @@
     )(jacobian, *small)
 
 
+def hand_over_kernel(energy_in, result_in, energy_out, result_out):
+    energy_out[...] = energy_in[...]
+    result_out[...] = result_in[...]
+
+
+def hand_over(energy, result):
+    return pl.pallas_call(
+        hand_over_kernel,
+        out_shape=[jax.ShapeDtypeStruct(x.shape, x.dtype) for x in (energy, result)],
+        compiler_params=pltpu.CompilerParams(vmem_limit_bytes=60 * 1024 * 1024),
+    )(energy, result)
+
+
 def finish_outside(n, rows, gram, cent, prev_update):
     walkers = n * rows
     along = gram[:, :rows, rows].reshape(walkers)
@@ -446,6 +459,7 @@
     )
     if cent:
         return (energy[:, 0], finish_outside(n, rows, result, cent[0], prev_update))
+    energy, result = hand_over(energy, result)
     return (energy.reshape(rows), result)
 
 

time: 35.8 us -> 35.3 us (0.986)
  local copies, waits for them, and re-layouts: 1.74 us -> 0 us
  Pallas kernels: 33.2 us -> 34.5 us
    unnamed x6 -> x0, local copies, waits for them, and re-layouts: 1.74 us -> none
    pallas_call x0 -> x1, Pallas kernels: none -> 1.27 us  [hand_over(): pl.pallas_call(hand_over_kernel, out_shape=[jax.ShapeDtypeStruct(x.shape,...]
where the time goes in v8:
time: 35.3 us; the launch traced here: 35.1 us
  Pallas kernels  34.5 us (98%)
  between operations  0.64 us (2%)
    pallas_call x1, Pallas kernels, step(): pl.pallas_call(functools.partial(step_kernel, n, m, finish), out_shape=[j...  33.2 us
    pallas_call x1, Pallas kernels, hand_over(): pl.pallas_call(hand_over_kernel, out_shape=[jax.ShapeDtypeStruct(x.shape,...  1.27 us

profile of v8, /device:TPU:0, one launch (start us, length us, event | category | flops | bytes accessed | tf_op | source)
XLA Modules:
  0.0 35.1 jit_solution(14266303906050397071)
XLA Ops:
  0.6 33.2 %shard_map.113 = (f32[1,6]{1,0:T(1,128)}, f32[1,1024]{1,0:T(1,128)}) custom-call(f32[6,16384]{1,0:T(8,128)} %jac_ref.1, f32[1,1024]{1,0:T(1,128)} %prev_ref.1, f32[1,6]{1,0:T(1,128)} %bitcast.9, f32[6,3,66]{2,1,0:T(4,128)} %elec_ref.1, f32[3,21]{1,0:T(4,128)} %atom_ref.1, f32[6,12,21,66]{3,2,1,0:T(8,128)} %bitcast.6, s32[6,66]{1,0:T(8,128)} %rotation_ref.1, ...), custom_call_target="tpu_custom_call" | custom-call | tf_op jit(solution)/shard_map/pallas_call | solution.py:381
  33.9 1.3 %shard_map.114 = (f32[1,6]{1,0:T(1,128)}, f32[1,1024]{1,0:T(1,128)}) custom-call(f32[1,6]{1,0:T(1,128)} %get-tuple-element.6.energy_in, f32[1,1024]{1,0:T(1,128)} %get-tuple-element.7.result_in), custom_call_target="tpu_custom_call" | custom-call | tf_op jit(solution)/shard_map/pallas_call | solution.py:408
